TPU v7x, 32 devices: a whole 2x2x4 slice. The times are simulated.
32 devices in a mesh: gx: 8 (over z, x), gy: 2 (over core), gz: 2 (over y).
Axes of the slice: x: 2, y: 2, z: 4, core: 2. Of those that a mesh axis runs over, the one named last changes fastest.
Arguments:
- velocity: bfloat16 [3, 16, 16, 256], P(None, 'gx', 'gy', 'gz'), may hold values from -6 to 6
- eddy_viscosity: float32 [16, 16, 256], P('gx', 'gy', 'gz'), may hold values from 0.02 to 0.3
- cell_owner: int32 [2, 2, 16384, 1], P('gy', 'gz', 'gx'), may hold values from 0 to 7; in each aligned block of 2048 rows (0 to 2047, 2048 to 4095, ..., all dimensions but the last counted through in order) at most 384 rows name the same one
- cell_element: int32 [2, 2, 16384], P('gy', 'gz', 'gx'), may hold values from 0 to 3
- cell_position: int32 [2, 2, 16384], P('gy', 'gz', 'gx'), may hold values from 0 to 4095
- acoustic_state: float32 [4, 8, 2, 8, 512], P(None, 'gx', 'gy', 'gz'), may hold values from -6 to 6
Outputs:
- source_moments: float32 [8, 2, 8, 3, 512], P('gx', 'gy', 'gz')
- next_state: float32 [4, 8, 2, 8, 512], P(None, 'gx', 'gy', 'gz')
Inputs may be any that keep to these rules, and one draw needn't show every extreme that they name: `cell_owner`: in the rows of one device (aligned blocks of 2048 rows along the last two dimensions), no owner is named more than 384 times, a bound that some block reaches.
All inputs are finite; a program needn't handle non-finite values.
Results may differ from a plain program's by a relative error of at most 0.0039.
Values may be sent and summed in bfloat16 or wider, within the bound.
A program may use at most 64 MiB of HBM per device.

v0:
```python
import jax
import jax.numpy as jnp
import numpy as np
from jax import lax
from jax.sharding import PartitionSpec as P

SUB = 16
NODES = 512


GLL_POINTS = np.array(
    [
        -1.0,
        -0.8717401485096066,
        -0.5917001814331423,
        -0.2092992179024789,
        0.2092992179024789,
        0.5917001814331423,
        0.8717401485096066,
        1.0,
    ]
)
LIFT_FACTOR = 28.0
TIME_STEP = 0.01
COUPLING = 4.0
MOMENT_WEIGHT = 0.0625


def extended(cells, sides, width):
    for axis, dim in sides:
        count = lax.axis_size(axis)
        ends = count - 1
        head = lax.slice_in_dim(cells, 0, width, axis=dim)
        tail = lax.slice_in_dim(cells, cells.shape[dim] - width, cells.shape[dim], axis=dim)
        cells = jnp.concatenate(
            [
                lax.ppermute(tail, axis, [(i, (i + 1) % count) for i in range(ends)]),
                cells,
                lax.ppermute(head, axis, [((i + 1) % count, i) for i in range(ends)]),
            ],
            axis=dim,
        )
    return cells


def derivative_matrix():
    points = GLL_POINTS
    barycentric = np.ones(8)
    for j in range(8):
        for m in range(8):
            if m != j:
                barycentric[j] = barycentric[j] / (points[j] - points[m])
    matrix = np.zeros((8, 8))
    for i in range(8):
        for j in range(8):
            if i != j:
                matrix[i, j] = barycentric[j] / barycentric[i] / (points[i] - points[j])
        matrix[i, i] = -np.sum(matrix[i])
    return matrix


def kron_tables():
    matrix = derivative_matrix()
    identity = np.eye(8)
    along_x = np.kron(np.kron(matrix, identity), identity).T
    along_y = np.kron(np.kron(identity, matrix), identity).T
    along_z = np.kron(np.kron(identity, identity), matrix).T
    return [jnp.asarray(t, dtype=jnp.float32) for t in (along_x, along_y, along_z)]


def basis_table():
    points = GLL_POINTS
    centres = -1.0 + (2.0 * np.arange(SUB) + 1.0) / SUB
    values = np.ones((SUB, 8))
    for j in range(8):
        for m in range(8):
            if m != j:
                values[:, j] = values[:, j] * (centres - points[m]) / (points[j] - points[m])
    return jnp.asarray(values, dtype=jnp.float32)


def source_from_padded(padded, viscosity):
    centre = padded[:, 1:-1, 1:-1, 1:-1]
    plus_x = padded[:, 2:, 1:-1, 1:-1]
    minus_x = padded[:, :-2, 1:-1, 1:-1]
    plus_y = padded[:, 1:-1, 2:, 1:-1]
    minus_y = padded[:, 1:-1, :-2, 1:-1]
    plus_z = padded[:, 1:-1, 1:-1, 2:]
    minus_z = padded[:, 1:-1, 1:-1, :-2]
    grad_x = 0.5 * (plus_x - minus_x)
    grad_y = 0.5 * (plus_y - minus_y)
    grad_z = 0.5 * (plus_z - minus_z)
    laplace = plus_x + minus_x + plus_y + minus_y + plus_z + minus_z - 6.0 * centre
    curl_x = grad_y[2] - grad_z[1]
    curl_y = grad_z[0] - grad_x[2]
    curl_z = grad_x[1] - grad_y[0]
    lamb_x = curl_y * centre[2] - curl_z * centre[1]
    lamb_y = curl_z * centre[0] - curl_x * centre[2]
    lamb_z = curl_x * centre[1] - curl_y * centre[0]
    lamb = jnp.stack([lamb_x, lamb_y, lamb_z])
    return (viscosity[None] * laplace - lamb).astype(jnp.bfloat16)


def face_correction(inside, outside, normal, component):
    difference = inside - outside
    result = -0.5 * difference
    result = result.at[0].add(0.5 * normal * difference[component])
    result = result.at[component].add(0.5 * normal * difference[0])
    return LIFT_FACTOR * result


def tendency(fields, forcing, tables, exterior):
    highest = lax.Precision.HIGHEST
    pressure = fields[0]
    grad_x = jnp.dot(pressure, tables[0], precision=highest)
    grad_y = jnp.dot(pressure, tables[1], precision=highest)
    grad_z = jnp.dot(pressure, tables[2], precision=highest)
    divergence = (
        jnp.dot(fields[1], tables[0], precision=highest)
        + jnp.dot(fields[2], tables[1], precision=highest)
        + jnp.dot(fields[3], tables[2], precision=highest)
    )
    result = jnp.stack(
        [
            -divergence,
            COUPLING * forcing[0] - grad_x,
            COUPLING * forcing[1] - grad_y,
            COUPLING * forcing[2] - grad_z,
        ]
    )
    shape_now = fields.shape
    nodal_view = fields.reshape(shape_now[:4] + (8, 8, 8))
    result = result.reshape(nodal_view.shape)
    for direction in range(3):
        node_axis = 4 + direction
        lower_face = jnp.take(nodal_view, 0, axis=node_axis)
        upper_face = jnp.take(nodal_view, 7, axis=node_axis)
        lower_outer, upper_outer = exterior(lower_face, upper_face, direction)
        leading = (slice(None),) * node_axis
        result = result.at[leading + (0,)].add(
            face_correction(lower_face, lower_outer, -1.0, direction + 1)
        )
        result = result.at[leading + (7,)].add(
            face_correction(upper_face, upper_outer, 1.0, direction + 1)
        )
    return result.reshape(shape_now)


def runge_kutta(fields, forcing, exterior):
    tables = kron_tables()
    section_one = fields + TIME_STEP * tendency(fields, forcing, tables, exterior)
    section_two = 0.75 * fields + 0.25 * (
        section_one + TIME_STEP * tendency(section_one, forcing, tables, exterior)
    )
    return 1.0 / 3.0 * fields + 2.0 / 3.0 * (
        section_two + TIME_STEP * tendency(section_two, forcing, tables, exterior)
    )


def halo_exterior(lower_face, upper_face, direction):
    elem_axis = direction + 1
    extent = lower_face.shape[elem_axis]
    sent_faces = jnp.concatenate(
        [
            lax.slice_in_dim(lower_face, 0, 1, axis=elem_axis),
            lax.slice_in_dim(upper_face, extent - 1, extent, axis=elem_axis),
        ],
        axis=elem_axis,
    )
    if direction == 0:
        padded = extended(sent_faces, (("gx", 1),), 1)
    elif direction == 1:
        padded = extended(sent_faces, (("gy", 2),), 1)
    else:
        padded = extended(sent_faces, (("gz", 3),), 1)
    from_below = lax.slice_in_dim(padded, 0, 1, axis=elem_axis)
    from_above = lax.slice_in_dim(padded, 3, 4, axis=elem_axis)
    lower_outer = jnp.concatenate(
        [from_below, lax.slice_in_dim(upper_face, 0, extent - 1, axis=elem_axis)], axis=elem_axis
    )
    upper_outer = jnp.concatenate(
        [lax.slice_in_dim(lower_face, 1, extent, axis=elem_axis), from_above], axis=elem_axis
    )
    return (lower_outer, upper_outer)


def basis_rows(positions, values):
    highest = lax.Precision.HIGHEST
    levels = jnp.arange(SUB, dtype=jnp.int32)[None, :]
    first_index = positions // (SUB * SUB)
    second_index = positions // SUB % SUB
    third_index = positions % SUB
    along_a = jnp.dot(
        (first_index[:, None] == levels).astype(jnp.float32), values, precision=highest
    )
    along_b = jnp.dot(
        (second_index[:, None] == levels).astype(jnp.float32), values, precision=highest
    )
    along_c = jnp.dot(
        (third_index[:, None] == levels).astype(jnp.float32), values, precision=highest
    )
    node_rows = along_a[:, :, None, None] * along_b[:, None, :, None] * along_c[:, None, None, :]
    return node_rows.reshape(positions.shape[0], NODES).astype(jnp.bfloat16)


def on_device(velocity, eddy_viscosity, cell_owner, cell_element, cell_position, acoustic_state):
    padded = extended(velocity, (("gx", 1), ("gy", 2), ("gz", 3)), 1)
    sources = source_from_padded(padded.astype(jnp.float32), eddy_viscosity)
    cell_count = sources.shape[1] * sources.shape[2] * sources.shape[3]
    flat_source = sources.reshape(3, cell_count)
    owners = cell_owner.reshape(cell_count)
    elements = cell_element.reshape(cell_count)
    positions = cell_position.reshape(cell_count)
    owner_count = lax.axis_size("gx")
    capacity = 3 * cell_count // (2 * owner_count)
    owner_hot = (owners[:, None] == jnp.arange(owner_count, dtype=jnp.int32)[None, :]).astype(
        jnp.int32
    )
    earlier = jnp.cumsum(owner_hot, axis=0) - owner_hot
    order_within = jnp.sum(earlier * owner_hot, axis=1)
    slot_index = owners * capacity + order_within
    send_source = (
        jnp.zeros((3, owner_count * capacity), jnp.bfloat16)
        .at[:, slot_index]
        .set(flat_source)
        .reshape(3, owner_count, capacity)
    )
    send_ids = (
        jnp.zeros((2, owner_count * capacity), jnp.int32)
        .at[:, slot_index]
        .set(jnp.stack([elements, positions]))
        .reshape(2, owner_count, capacity)
    )
    got_source, got_ids = (
        lax.all_to_all(send_source, "gx", split_axis=1, concat_axis=1, tiled=True),
        lax.all_to_all(send_ids, "gx", split_axis=1, concat_axis=1, tiled=True),
    )
    local_elems = acoustic_state.shape[1] * acoustic_state.shape[2] * acoustic_state.shape[3]
    senders = 8
    width_rows = senders * capacity
    values = basis_table()

    def accumulate(step_index, totals):
        piece_source = lax.dynamic_slice_in_dim(
            got_source, step_index * senders, senders, 1
        ).reshape(3, width_rows)
        piece_ids = lax.dynamic_slice_in_dim(got_ids, step_index * senders, senders, 1)
        piece_element = piece_ids[0].reshape(width_rows)
        piece_position = piece_ids[1].reshape(width_rows)
        node_rows = basis_rows(piece_position, values)
        element_hot = (
            jnp.arange(local_elems, dtype=jnp.int32)[:, None] == piece_element[None, :]
        ).astype(jnp.bfloat16)
        weighted = (element_hot[None, :, :] * piece_source[:, None, :]).reshape(
            3 * local_elems, width_rows
        )
        return totals + jnp.dot(weighted, node_rows, preferred_element_type=jnp.float32)

    totals = lax.fori_loop(
        0, owner_count // senders, accumulate, jnp.zeros((3 * local_elems, NODES), jnp.float32)
    )
    forcing = (totals * MOMENT_WEIGHT).reshape(
        3, acoustic_state.shape[1], acoustic_state.shape[2], acoustic_state.shape[3], NODES
    )
    moments = jnp.moveaxis(forcing, 0, 3)
    next_state = runge_kutta(acoustic_state, forcing, halo_exterior)
    return (moments, next_state)


def solution(mesh):
    in_specs = (
        P(None, "gx", "gy", "gz"),
        P("gx", "gy", "gz"),
        P("gy", "gz", "gx", None),
        P("gy", "gz", "gx"),
        P("gy", "gz", "gx"),
        P(None, "gx", "gy", "gz", None),
    )
    out_specs = (P("gx", "gy", "gz", None, None), P(None, "gx", "gy", "gz", None))
    return jax.shard_map(
        on_device, mesh=mesh, in_specs=in_specs, out_specs=out_specs, check_vma=False
    )
```

profile of v0, /device:TPU:0, one launch (start us, length us, event | category | flops | bytes accessed | tf_op | source)
XLA Modules:
  0.0 267.1 jit_solution(6777456949243246022)
XLA Ops:
  2.0 5.4 %collective-permute-start = (bf16[3,1,8,128]{3,2,1,0:T(8,128)(2,1)}, bf16[3,1,8,128]{3,2,1,0:T(8,128)(2,1)}, u32[]{:S(2)}, u32[]{:S(2)}) collective-permute-start(bf16[3,1,8,128]{3,2,1,0:T(8,128)(2,1)} %get-tuple-element.832), channel_id=1, source_target_pairs={{0,4},{4,8},{8,12},{12,16},{16,20},{20,24},{24,28},{1,5},{5,9},{9,... | collective-permute-start | bytes 18440 | tf_op jit(solution)/shard_map/ppermute | solution.py:37
  9.4 2.3 reduce-window.6
  14.8 6.8 %scatter_custom_fusion = s32[2,3072]{0,1:T(8,128)} fusion(s32[2048]{0:T(1024)S(1)} %bitcast.472, s32[2048,2]{1,0:T(8,128)S(1)} %copy.773, s32[]{:T(128)} %constant.1307.clone.1), kind=kCustom, calls=%fused_computation.26 | custom fusion | bytes 24580 | tf_op jit(solution)/shard_map/scatter | solution.py:231
  21.6 2.6 copy.774
  24.2 6.4 %all-to-all-start = ((s32[2,8,384]{2,0,1:T(2,128)}), s32[2,8,384]{2,0,1:T(2,128)}, u32[]{:S(2)}, u32[]{:S(2)}) async-start(s32[2,8,384]{2,0,1:T(2,128)} %copy.774), calls=%async_computation | async-start | bytes 49152 | tf_op jit(solution)/shard_map/all_to_all | solution.py:236
  33.3 4.5 %collective-permute-start.6 = (f32[4,1,1,4,8,8]{4,3,0,5,2,1:T(4,128)}, f32[4,1,1,4,8,8]{4,3,0,5,2,1:T(4,128)}, u32[]{:S(2)}, u32[]{:S(2)}) collective-permute-start(f32[4,1,1,4,8,8]{4,3,0,5,2,1:T(4,128)} %bitcast.30), channel_id=1, source_target_pairs={{0,4},{4,8},{8,12},{12,16},{16,20},{20,24},{24,28},{1,5},{5,9},{9,... | collective-permute-start | bytes 12296 | tf_op jit(solution)/shard_map/ppermute | solution.py:37
  41.6 3.4 %collective-permute-start.10 = (f32[4,1,1,1,8,8]{5,4,3,0,2,1:T(8,128)S(1)}, f32[4,1,1,1,8,8]{5,4,3,0,2,1:T(8,128)S(1)}, u32[]{:S(2)}, u32[]{:S(2)}) collective-permute-start(f32[4,1,1,1,8,8]{5,4,3,0,2,1:T(8,128)S(1)} %slice.2703), channel_id=1, source_target_pairs={{0,1},{2,3},{4,5},{6,7},{8,9},{10,11},{12,13},{14,15},{16,17},{18,... | collective-permute-start | bytes 3080 | tf_op jit(solution)/shard_map/ppermute | solution.py:37
  53.2 3.5 %collective-permute-done.11 = f32[4,1,1,1,8,8]{5,4,3,0,2,1:T(8,128)S(1)} collective-permute-done((f32[4,1,1,1,8,8]{5,4,3,0,2,1:T(8,128)S(1)}, f32[4,1,1,1,8,8]{5,4,3,0,2,1:T(8,128)S(1)}, u32[]{:S(2)}, u32[]{:S(2)}) %collective-permute-start.11) | collective-permute-done | bytes 1056 | tf_op jit(solution)/shard_map/ppermute | solution.py:39
  66.7 3.7 %collective-permute-start.2 = (bf16[3,4,1,128]{3,2,1,0:T(2,128)(2,1)S(1)}, bf16[3,4,1,128]{3,2,1,0:T(2,128)(2,1)S(1)}, u32[]{:S(2)}, u32[]{:S(2)}) collective-permute-start(bf16[3,4,1,128]{3,2,1,0:T(2,128)(2,1)S(1)} %get-tuple-element.826), channel_id=1, source_target_pairs={{0,2},{1,3},{4,6},{5,7},{8,10},{9,11},{12,14},{13,15},{16,18},{17,... | collective-permute-start | bytes 9224 | tf_op jit(solution)/shard_map/ppermute | solution.py:37
  84.3 7.0 %scatter_custom_fusion.1 = bf16[3,3072]{0,1:T(8,128)(2,1)} fusion(s32[2048]{0:T(1024)} %bitcast.473, bf16[2048,3]{1,0:T(8,128)(2,1)} %bitcast.449, bf16[]{:T(256)} %constant.1310.clone.1), kind=kCustom, calls=%fused_computation.59 | custom fusion | bytes 18944 | tf_op jit(solution)/shard_map/scatter | solution.py:225
  93.4 6.6 %all-to-all-start.1 = ((bf16[3,8,384]{2,0,1:T(4,128)(2,1)}), bf16[3,8,384]{2,0,1:T(4,128)(2,1)S(1)}, u32[]{:S(2)}, u32[]{:S(2)}) async-start(bf16[3,8,384]{2,0,1:T(4,128)(2,1)} %copy.776), calls=%async_computation.1 | async-start | bytes 49152 | tf_op jit(solution)/shard_map/all_to_all | solution.py:235
  100.9 5.8 %all-to-all-done.1 = bf16[3,8,384]{2,0,1:T(4,128)(2,1)S(1)} async-done(((bf16[3,8,384]{2,0,1:T(4,128)(2,1)}), bf16[3,8,384]{2,0,1:T(4,128)(2,1)S(1)}, u32[]{:S(2)}, u32[]{:S(2)}) %all-to-all-start.1) | async-done | bytes 18464 | tf_op jit(solution)/shard_map/all_to_all | solution.py:235
  117.9 2.9 %scatter-add.184 = f32[4,1,1,4,8,8,8]{5,4,3,0,6,2,1:T(8,128)} dynamic-update-slice(f32[4,1,1,4,8,8,8]{5,4,3,0,6,2,1:T(8,128)} %copy-done.3, f32[4,1,1,4,1,8,8]{5,4,3,0,6,2,1:T(1,128)S(1)} %slice_add_fusion.8, s32[]{:T(128)} %constant.1307.clone.1, s32[]{:T(128)} %constant.1307.clone.1, s32[]{:T(128)} %constant.1307.clone.1, s32[]{:T(128)} %constant.1307.clone.1, s32[]{:T(128)} %constant.1307.clone.1, ...) | dynamic-update-slice | bytes 8196 | tf_op jit(solution)/shard_map/scatter-add | solution.py:140
  121.9 2.9 %scatter-add.189 = f32[4,1,1,4,8,8,8]{5,4,3,0,6,2,1:T(8,128)} dynamic-update-slice(f32[4,1,1,4,8,8,8]{5,4,3,0,6,2,1:T(8,128)} %scatter-add.184, f32[4,1,1,4,1,8,8]{5,4,3,0,6,2,1:T(1,128)S(1)} %slice_add_fusion.7, s32[]{:T(128)} %constant.1307.clone.1, s32[]{:T(128)} %constant.1307.clone.1, s32[]{:T(128)} %constant.1307.clone.1, s32[]{:T(128)} %constant.1307.clone.1, s32[]{:T(128)} %constant.1324.clone.1, ...) | dynamic-update-slice | bytes 8196 | tf_op jit(solution)/shard_map/scatter-add | solution.py:143
  124.8 2.1 slice_add_fusion.1
  126.8 3.0 %scatter-add.194 = f32[4,1,1,4,8,8,8]{5,4,3,0,6,2,1:T(8,128)} dynamic-update-slice(f32[4,1,1,4,8,8,8]{5,4,3,0,6,2,1:T(8,128)} %scatter-add.189, f32[4,1,1,4,8,1,8]{5,4,3,0,6,2,1:T(8,128)} %slice_add_fusion.1, s32[]{:T(128)} %constant.1307.clone.1, s32[]{:T(128)} %constant.1307.clone.1, s32[]{:T(128)} %constant.1307.clone.1, s32[]{:T(128)} %constant.1307.clone.1, s32[]{:T(128)} %constant.1307.clone.1, ...) | dynamic-update-slice | bytes 8196 | tf_op jit(solution)/shard_map/scatter-add | solution.py:140
  129.8 2.2 slice_add_fusion
  132.0 11.8 %scatter-add.199 = f32[4,1,1,4,8,8,8]{5,4,3,0,6,2,1:T(8,128)} dynamic-update-slice(f32[4,1,1,4,8,8,8]{5,4,3,0,6,2,1:T(8,128)} %scatter-add.194, f32[4,1,1,4,8,1,8]{5,4,3,0,6,2,1:T(8,128)} %slice_add_fusion, s32[]{:T(128)} %constant.1307.clone.1, s32[]{:T(128)} %constant.1307.clone.1, s32[]{:T(128)} %constant.1307.clone.1, s32[]{:T(128)} %constant.1307.clone.1, s32[]{:T(128)} %constant.1307.clone.1, ...) | dynamic-update-slice | bytes 8196 | tf_op jit(solution)/shard_map/scatter-add | solution.py:143
  148.7 2.1 copy.810
  153.3 2.4 fusion.157
  170.9 5.7 %collective-permute-start.16 = (f32[4,1,1,1,8,8]{5,4,3,0,2,1:T(8,128)}, f32[4,1,1,1,8,8]{5,4,3,0,2,1:T(8,128)}, u32[]{:S(2)}, u32[]{:S(2)}) collective-permute-start(f32[4,1,1,1,8,8]{5,4,3,0,2,1:T(8,128)} %slice.2747), channel_id=1, source_target_pairs={{0,1},{2,3},{4,5},{6,7},{8,9},{10,11},{12,13},{14,15},{16,17},{18,... | collective-permute-start | bytes 3080 | tf_op jit(solution)/shard_map/ppermute | solution.py:37
  177.9 4.3 %collective-permute-start.14 = (f32[4,1,1,4,8,8]{5,4,3,0,2,1:T(8,128)}, f32[4,1,1,4,8,8]{5,4,3,0,2,1:T(8,128)}, u32[]{:S(2)}, u32[]{:S(2)}) collective-permute-start(f32[4,1,1,4,8,8]{5,4,3,0,2,1:T(8,128)} %bitcast.66), channel_id=1, source_target_pairs={{0,2},{1,3},{4,6},{5,7},{8,10},{9,11},{12,14},{13,15},{16,18},{17,... | collective-permute-start | bytes 12296 | tf_op jit(solution)/shard_map/ppermute | solution.py:37
  182.1 3.0 %collective-permute-start.12 = (f32[4,1,1,4,8,8]{5,4,3,0,2,1:T(8,128)}, f32[4,1,1,4,8,8]{5,4,3,0,2,1:T(8,128)}, u32[]{:S(2)}, u32[]{:S(2)}) collective-permute-start(f32[4,1,1,4,8,8]{5,4,3,0,2,1:T(8,128)} %get-tuple-element.814), channel_id=1, source_target_pairs={{0,4},{4,8},{8,12},{12,16},{16,20},{20,24},{24,28},{1,5},{5,9},{9,... | collective-permute-start | bytes 12296 | tf_op jit(solution)/shard_map/ppermute | solution.py:37
  201.6 2.9 %scatter-add.224 = f32[4,1,1,4,8,8,8]{6,5,3,0,4,2,1:T(8,128)} dynamic-update-slice(f32[4,1,1,4,8,8,8]{6,5,3,0,4,2,1:T(8,128)} %copy-done.4, f32[4,1,1,4,8,1,8]{6,5,3,0,4,2,1:T(1,128)S(1)} %slice_add_fusion.6, s32[]{:T(128)} %constant.1307.clone.1, s32[]{:T(128)} %constant.1307.clone.1, s32[]{:T(128)} %constant.1307.clone.1, s32[]{:T(128)} %constant.1307.clone.1, s32[]{:T(128)} %constant.1307.clone.1, ...) | dynamic-update-slice | bytes 8196 | tf_op jit(solution)/shard_map/scatter-add | solution.py:140
  205.6 2.9 %scatter-add.229 = f32[4,1,1,4,8,8,8]{6,5,3,0,4,2,1:T(8,128)} dynamic-update-slice(f32[4,1,1,4,8,8,8]{6,5,3,0,4,2,1:T(8,128)} %scatter-add.224, f32[4,1,1,4,8,1,8]{6,5,3,0,4,2,1:T(1,128)S(1)} %slice_add_fusion.5, s32[]{:T(128)} %constant.1307.clone.1, s32[]{:T(128)} %constant.1307.clone.1, s32[]{:T(128)} %constant.1307.clone.1, s32[]{:T(128)} %constant.1307.clone.1, s32[]{:T(128)} %constant.1307.clone.1, ...) | dynamic-update-slice | bytes 8196 | tf_op jit(solution)/shard_map/scatter-add | solution.py:143
  208.5 2.2 copy.839
  216.5 2.1 copy.844
  221.1 2.3 fusion.154
  233.1 4.5 %collective-permute-start.22 = (f32[4,1,1,1,8,8]{5,4,3,0,2,1:T(8,128)S(1)}, f32[4,1,1,1,8,8]{5,4,3,0,2,1:T(8,128)S(1)}, u32[]{:S(2)}, u32[]{:S(2)}) collective-permute-start(f32[4,1,1,1,8,8]{5,4,3,0,2,1:T(8,128)S(1)} %slice.2791), channel_id=1, source_target_pairs={{0,1},{2,3},{4,5},{6,7},{8,9},{10,11},{12,13},{14,15},{16,17},{18,... | collective-permute-start | bytes 3080 | tf_op jit(solution)/shard_map/ppermute | solution.py:37
  238.9 3.0 %collective-permute-start.20 = (f32[4,1,1,4,8,8]{5,4,3,0,2,1:T(8,128)S(1)}, f32[4,1,1,4,8,8]{5,4,3,0,2,1:T(8,128)S(1)}, u32[]{:S(2)}, u32[]{:S(2)}) collective-permute-start(f32[4,1,1,4,8,8]{5,4,3,0,2,1:T(8,128)S(1)} %bitcast.456), channel_id=1, source_target_pairs={{0,2},{1,3},{4,6},{5,7},{8,10},{9,11},{12,14},{13,15},{16,18},{17,... | collective-permute-start | bytes 12296 | tf_op jit(solution)/shard_map/ppermute | solution.py:37
  245.5 4.8 %collective-permute-start.18 = (f32[4,1,1,4,8,8]{5,3,0,4,2,1:T(4,128)S(1)}, f32[4,1,1,4,8,8]{5,3,0,4,2,1:T(4,128)S(1)}, u32[]{:S(2)}, u32[]{:S(2)}) collective-permute-start(f32[4,1,1,4,8,8]{5,3,0,4,2,1:T(4,128)S(1)} %bitcast.466), channel_id=1, source_target_pairs={{0,4},{4,8},{8,12},{12,16},{16,20},{20,24},{24,28},{1,5},{5,9},{9,... | collective-permute-start | bytes 12296 | tf_op jit(solution)/shard_map/ppermute | solution.py:37
  255.4 10.3 %scatter-add.259 = f32[4,1,1,4,8,8,8]{5,4,3,0,6,2,1:T(8,128)S(1)} dynamic-update-slice(f32[4,1,1,4,8,8,8]{5,4,3,0,6,2,1:T(8,128)S(1)} %copy.869, f32[4,1,1,4,8,1,8]{5,4,3,0,6,2,1:T(8,128)S(1)} %copy.870, s32[]{:T(128)} %constant.1307.clone.1, s32[]{:T(128)} %constant.1307.clone.1, s32[]{:T(128)} %constant.1307.clone.1, s32[]{:T(128)} %constant.1307.clone.1, s32[]{:T(128)} %constant.1307.clone.1, ...) | dynamic-update-slice | bytes 8196 | tf_op jit(solution)/shard_map/scatter-add | solution.py:143
  (263 shorter events, 129.9 us)
Async XLA Ops:
  0.6 30.0 %copy-start.5 = (f32[4,1,1,4,512]{4,3,2,1,0:T(4,128)S(1)}, f32[4,1,1,4,512]{4,3,2,1,0:T(4,128)}, u32[]{:S(2)}) copy-start(f32[4,1,1,4,512]{4,3,2,1,0:T(4,128)} %param.135) | copy-start | bytes 98308
  2.0 63.3 %collective-permute-start = (bf16[3,1,8,128]{3,2,1,0:T(8,128)(2,1)}, bf16[3,1,8,128]{3,2,1,0:T(8,128)(2,1)}, u32[]{:S(2)}, u32[]{:S(2)}) collective-permute-start(bf16[3,1,8,128]{3,2,1,0:T(8,128)(2,1)} %get-tuple-element.832), channel_id=1, source_target_pairs={{0,4},{4,8},{8,12},{12,16},{16,20},{20,24},{24,28},{1,5},{5,9},{9,... | collective-permute-start | bytes 18440 | tf_op jit(solution)/shard_map/ppermute | solution.py:37
  7.4 59.3 %collective-permute-start.1 = (bf16[3,1,8,128]{3,2,1,0:T(8,128)(2,1)}, bf16[3,1,8,128]{3,2,1,0:T(8,128)(2,1)S(1)}, u32[]{:S(2)}, u32[]{:S(2)}) collective-permute-start(bf16[3,1,8,128]{3,2,1,0:T(8,128)(2,1)} %get-tuple-element.831), channel_id=1, source_target_pairs={{4,0},{8,4},{12,8},{16,12},{20,16},{24,20},{28,24},{5,1},{9,5},{13... | collective-permute-start | bytes 18440 | tf_op jit(solution)/shard_map/ppermute | solution.py:39
  13.6 27.9 %copy-start.10 = (s32[2048,1]{0,1:T(1,128)}, s32[2048,1]{0,1:T(1,128)S(1)}, u32[]{:S(2)}) copy-start(s32[2048,1]{0,1:T(1,128)S(1)} %compare_select_fusion) | copy-start | bytes 24580
  14.4 30.6 %copy-start.2 = (f32[512,512]{1,0:T(8,128)S(1)}, f32[512,512]{1,0:T(8,128)}, u32[]{:S(2)}) copy-start(f32[512,512]{1,0:T(8,128)} %constant.1333.clone) | copy-start | bytes 3145732
  14.8 30.9 %copy-start.1 = (f32[512,512]{1,0:T(8,128)S(1)}, f32[512,512]{1,0:T(8,128)}, u32[]{:S(2)}) copy-start(f32[512,512]{1,0:T(8,128)} %constant.1334.clone) | copy-start | bytes 3145732
  24.2 69.2 %all-to-all-start = ((s32[2,8,384]{2,0,1:T(2,128)}), s32[2,8,384]{2,0,1:T(2,128)}, u32[]{:S(2)}, u32[]{:S(2)}) async-start(s32[2,8,384]{2,0,1:T(2,128)} %copy.774), calls=%async_computation | async-start | bytes 49152 | tf_op jit(solution)/shard_map/all_to_all | solution.py:236
  33.3 25.6 %collective-permute-start.6 = (f32[4,1,1,4,8,8]{4,3,0,5,2,1:T(4,128)}, f32[4,1,1,4,8,8]{4,3,0,5,2,1:T(4,128)}, u32[]{:S(2)}, u32[]{:S(2)}) collective-permute-start(f32[4,1,1,4,8,8]{4,3,0,5,2,1:T(4,128)} %bitcast.30), channel_id=1, source_target_pairs={{0,4},{4,8},{8,12},{12,16},{16,20},{20,24},{24,28},{1,5},{5,9},{9,... | collective-permute-start | bytes 12296 | tf_op jit(solution)/shard_map/ppermute | solution.py:37
  38.5 23.2 %collective-permute-start.7 = (f32[4,1,1,4,8,8]{4,3,0,5,2,1:T(4,128)}, f32[4,1,1,4,8,8]{4,3,0,5,2,1:T(4,128)}, u32[]{:S(2)}, u32[]{:S(2)}) collective-permute-start(f32[4,1,1,4,8,8]{4,3,0,5,2,1:T(4,128)} %bitcast.29), channel_id=1, source_target_pairs={{4,0},{8,4},{12,8},{16,12},{20,16},{24,20},{28,24},{5,1},{9,5},{13... | collective-permute-start | bytes 12296 | tf_op jit(solution)/shard_map/ppermute | solution.py:39
  41.6 9.5 %collective-permute-start.10 = (f32[4,1,1,1,8,8]{5,4,3,0,2,1:T(8,128)S(1)}, f32[4,1,1,1,8,8]{5,4,3,0,2,1:T(8,128)S(1)}, u32[]{:S(2)}, u32[]{:S(2)}) collective-permute-start(f32[4,1,1,1,8,8]{5,4,3,0,2,1:T(8,128)S(1)} %slice.2703), channel_id=1, source_target_pairs={{0,1},{2,3},{4,5},{6,7},{8,9},{10,11},{12,13},{14,15},{16,17},{18,... | collective-permute-start | bytes 3080 | tf_op jit(solution)/shard_map/ppermute | solution.py:37
  51.1 5.6 %collective-permute-start.11 = (f32[4,1,1,1,8,8]{5,4,3,0,2,1:T(8,128)S(1)}, f32[4,1,1,1,8,8]{5,4,3,0,2,1:T(8,128)S(1)}, u32[]{:S(2)}, u32[]{:S(2)}) collective-permute-start(f32[4,1,1,1,8,8]{5,4,3,0,2,1:T(8,128)S(1)} %slice.2711), channel_id=1, source_target_pairs={{1,0},{3,2},{5,4},{7,6},{9,8},{11,10},{13,12},{15,14},{17,16},{19,... | collective-permute-start | bytes 3080 | tf_op jit(solution)/shard_map/ppermute | solution.py:39
  56.7 6.7 %collective-permute-start.8 = (f32[4,1,1,4,8,8]{5,4,3,0,2,1:T(8,128)}, f32[4,1,1,4,8,8]{5,4,3,0,2,1:T(8,128)S(1)}, u32[]{:S(2)}, u32[]{:S(2)}) collective-permute-start(f32[4,1,1,4,8,8]{5,4,3,0,2,1:T(8,128)} %bitcast.458), channel_id=1, source_target_pairs={{0,2},{1,3},{4,6},{5,7},{8,10},{9,11},{12,14},{13,15},{16,18},{17,... | collective-permute-start | bytes 12296 | tf_op jit(solution)/shard_map/ppermute | solution.py:37
  58.9 5.5 %collective-permute-start.9 = (f32[4,1,1,4,8,8]{5,4,3,0,2,1:T(8,128)}, f32[4,1,1,4,8,8]{5,4,3,0,2,1:T(8,128)}, u32[]{:S(2)}, u32[]{:S(2)}) collective-permute-start(f32[4,1,1,4,8,8]{5,4,3,0,2,1:T(8,128)} %bitcast.460), channel_id=1, source_target_pairs={{2,0},{3,1},{6,4},{7,5},{10,8},{11,9},{14,12},{15,13},{18,16},{19,... | collective-permute-start | bytes 12296 | tf_op jit(solution)/shard_map/ppermute | solution.py:39
  64.3 42.5 %copy-start.9 = (f32[16,8]{1,0:T(8,128)S(1)}, f32[16,8]{1,0:T(8,128)}, u32[]{:S(2)}) copy-start(f32[16,8]{1,0:T(8,128)} %constant.1332.clone) | copy-start | bytes 1540
  66.7 5.0 %collective-permute-start.2 = (bf16[3,4,1,128]{3,2,1,0:T(2,128)(2,1)S(1)}, bf16[3,4,1,128]{3,2,1,0:T(2,128)(2,1)S(1)}, u32[]{:S(2)}, u32[]{:S(2)}) collective-permute-start(bf16[3,4,1,128]{3,2,1,0:T(2,128)(2,1)S(1)} %get-tuple-element.826), channel_id=1, source_target_pairs={{0,2},{1,3},{4,6},{5,7},{8,10},{9,11},{12,14},{13,15},{16,18},{17,... | collective-permute-start | bytes 9224 | tf_op jit(solution)/shard_map/ppermute | solution.py:37
  70.4 3.1 %collective-permute-start.3 = (bf16[3,4,1,128]{3,2,1,0:T(2,128)(2,1)S(1)}, bf16[3,4,1,128]{3,2,1,0:T(2,128)(2,1)S(1)}, u32[]{:S(2)}, u32[]{:S(2)}) collective-permute-start(bf16[3,4,1,128]{3,2,1,0:T(2,128)(2,1)S(1)} %get-tuple-element.827), channel_id=1, source_target_pairs={{2,0},{3,1},{6,4},{7,5},{10,8},{11,9},{14,12},{15,13},{18,16},{19,... | collective-permute-start | bytes 9224 | tf_op jit(solution)/shard_map/ppermute | solution.py:39
  74.2 7.7 %collective-permute-start.4 = (bf16[3,4,10,1]{3,2,1,0:T(8,128)(2,1)}, bf16[3,4,10,1]{3,2,1,0:T(8,128)(2,1)S(1)}, u32[]{:S(2)}, u32[]{:S(2)}) collective-permute-start(bf16[3,4,10,1]{3,2,1,0:T(8,128)(2,1)} %get-tuple-element.822), channel_id=1, source_target_pairs={{0,1},{2,3},{4,5},{6,7},{8,9},{10,11},{12,13},{14,15},{16,17},{18,... | collective-permute-start | bytes 728 | tf_op jit(solution)/shard_map/ppermute | solution.py:37
  75.8 6.2 %collective-permute-start.5 = (bf16[3,4,10,1]{3,2,1,0:T(8,128)(2,1)}, bf16[3,4,10,1]{3,2,1,0:T(8,128)(2,1)S(1)}, u32[]{:S(2)}, u32[]{:S(2)}) collective-permute-start(bf16[3,4,10,1]{3,2,1,0:T(8,128)(2,1)} %get-tuple-element.823), channel_id=1, source_target_pairs={{1,0},{3,2},{5,4},{7,6},{9,8},{11,10},{13,12},{15,14},{17,16},{19,... | collective-permute-start | bytes 728 | tf_op jit(solution)/shard_map/ppermute | solution.py:39
  93.4 13.3 %all-to-all-start.1 = ((bf16[3,8,384]{2,0,1:T(4,128)(2,1)}), bf16[3,8,384]{2,0,1:T(4,128)(2,1)S(1)}, u32[]{:S(2)}, u32[]{:S(2)}) async-start(bf16[3,8,384]{2,0,1:T(4,128)(2,1)} %copy.776), calls=%async_computation.1 | async-start | bytes 49152 | tf_op jit(solution)/shard_map/all_to_all | solution.py:235
  116.2 29.2 %copy-start.8 = (f32[4,1,1,4,8,8]{5,4,3,0,2,1:T(8,128)S(1)}, f32[4,1,1,4,8,8]{5,4,3,0,2,1:T(8,128)}, u32[]{:S(2)}) copy-start(f32[4,1,1,4,8,8]{5,4,3,0,2,1:T(8,128)} %copy-done.7) | copy-start | bytes 12292
  169.6 23.7 %collective-permute-start.17 = (f32[4,1,1,1,8,8]{5,4,3,0,2,1:T(8,128)}, f32[4,1,1,1,8,8]{5,4,3,0,2,1:T(8,128)}, u32[]{:S(2)}, u32[]{:S(2)}) collective-permute-start(f32[4,1,1,1,8,8]{5,4,3,0,2,1:T(8,128)} %slice.2755), channel_id=1, source_target_pairs={{1,0},{3,2},{5,4},{7,6},{9,8},{11,10},{13,12},{15,14},{17,16},{19,... | collective-permute-start | bytes 3080 | tf_op jit(solution)/shard_map/ppermute | solution.py:39
  170.9 24.6 %collective-permute-start.16 = (f32[4,1,1,1,8,8]{5,4,3,0,2,1:T(8,128)}, f32[4,1,1,1,8,8]{5,4,3,0,2,1:T(8,128)}, u32[]{:S(2)}, u32[]{:S(2)}) collective-permute-start(f32[4,1,1,1,8,8]{5,4,3,0,2,1:T(8,128)} %slice.2747), channel_id=1, source_target_pairs={{0,1},{2,3},{4,5},{6,7},{8,9},{10,11},{12,13},{14,15},{16,17},{18,... | collective-permute-start | bytes 3080 | tf_op jit(solution)/shard_map/ppermute | solution.py:37
  176.6 19.6 %collective-permute-start.15 = (f32[4,1,1,4,8,8]{5,4,3,0,2,1:T(8,128)}, f32[4,1,1,4,8,8]{5,4,3,0,2,1:T(8,128)}, u32[]{:S(2)}, u32[]{:S(2)}) collective-permute-start(f32[4,1,1,4,8,8]{5,4,3,0,2,1:T(8,128)} %bitcast.65), channel_id=1, source_target_pairs={{2,0},{3,1},{6,4},{7,5},{10,8},{11,9},{14,12},{15,13},{18,16},{19,... | collective-permute-start | bytes 12296 | tf_op jit(solution)/shard_map/ppermute | solution.py:39
  177.9 19.3 %collective-permute-start.14 = (f32[4,1,1,4,8,8]{5,4,3,0,2,1:T(8,128)}, f32[4,1,1,4,8,8]{5,4,3,0,2,1:T(8,128)}, u32[]{:S(2)}, u32[]{:S(2)}) collective-permute-start(f32[4,1,1,4,8,8]{5,4,3,0,2,1:T(8,128)} %bitcast.66), channel_id=1, source_target_pairs={{0,2},{1,3},{4,6},{5,7},{8,10},{9,11},{12,14},{13,15},{16,18},{17,... | collective-permute-start | bytes 12296 | tf_op jit(solution)/shard_map/ppermute | solution.py:37
  182.1 16.0 %collective-permute-start.12 = (f32[4,1,1,4,8,8]{5,4,3,0,2,1:T(8,128)}, f32[4,1,1,4,8,8]{5,4,3,0,2,1:T(8,128)}, u32[]{:S(2)}, u32[]{:S(2)}) collective-permute-start(f32[4,1,1,4,8,8]{5,4,3,0,2,1:T(8,128)} %get-tuple-element.814), channel_id=1, source_target_pairs={{0,4},{4,8},{8,12},{12,16},{16,20},{20,24},{24,28},{1,5},{5,9},{9,... | collective-permute-start | bytes 12296 | tf_op jit(solution)/shard_map/ppermute | solution.py:37
  193.3 6.4 %collective-permute-start.13 = (f32[4,1,1,4,8,8]{5,4,3,0,2,1:T(8,128)}, f32[4,1,1,4,8,8]{5,4,3,0,2,1:T(8,128)S(1)}, u32[]{:S(2)}, u32[]{:S(2)}) collective-permute-start(f32[4,1,1,4,8,8]{5,4,3,0,2,1:T(8,128)} %get-tuple-element.813), channel_id=1, source_target_pairs={{4,0},{8,4},{12,8},{16,12},{20,16},{24,20},{28,24},{5,1},{9,5},{13... | collective-permute-start | bytes 12296 | tf_op jit(solution)/shard_map/ppermute | solution.py:39
  229.9 15.6 %collective-permute-start.23 = (f32[4,1,1,1,8,8]{5,4,3,0,2,1:T(8,128)S(1)}, f32[4,1,1,1,8,8]{5,4,3,0,2,1:T(8,128)S(1)}, u32[]{:S(2)}, u32[]{:S(2)}) collective-permute-start(f32[4,1,1,1,8,8]{5,4,3,0,2,1:T(8,128)S(1)} %slice.2799), channel_id=1, source_target_pairs={{1,0},{3,2},{5,4},{7,6},{9,8},{11,10},{13,12},{15,14},{17,16},{19,... | collective-permute-start | bytes 3080 | tf_op jit(solution)/shard_map/ppermute | solution.py:39
  233.1 17.3 %collective-permute-start.22 = (f32[4,1,1,1,8,8]{5,4,3,0,2,1:T(8,128)S(1)}, f32[4,1,1,1,8,8]{5,4,3,0,2,1:T(8,128)S(1)}, u32[]{:S(2)}, u32[]{:S(2)}) collective-permute-start(f32[4,1,1,1,8,8]{5,4,3,0,2,1:T(8,128)S(1)} %slice.2791), channel_id=1, source_target_pairs={{0,1},{2,3},{4,5},{6,7},{8,9},{10,11},{12,13},{14,15},{16,17},{18,... | collective-permute-start | bytes 3080 | tf_op jit(solution)/shard_map/ppermute | solution.py:37
  237.6 12.8 %collective-permute-start.21 = (f32[4,1,1,4,8,8]{5,4,3,0,2,1:T(8,128)S(1)}, f32[4,1,1,4,8,8]{5,4,3,0,2,1:T(8,128)S(1)}, u32[]{:S(2)}, u32[]{:S(2)}) collective-permute-start(f32[4,1,1,4,8,8]{5,4,3,0,2,1:T(8,128)S(1)} %bitcast.454), channel_id=1, source_target_pairs={{2,0},{3,1},{6,4},{7,5},{10,8},{11,9},{14,12},{15,13},{18,16},{19,... | collective-permute-start | bytes 12296 | tf_op jit(solution)/shard_map/ppermute | solution.py:39
  238.9 13.1 %collective-permute-start.20 = (f32[4,1,1,4,8,8]{5,4,3,0,2,1:T(8,128)S(1)}, f32[4,1,1,4,8,8]{5,4,3,0,2,1:T(8,128)S(1)}, u32[]{:S(2)}, u32[]{:S(2)}) collective-permute-start(f32[4,1,1,4,8,8]{5,4,3,0,2,1:T(8,128)S(1)} %bitcast.456), channel_id=1, source_target_pairs={{0,2},{1,3},{4,6},{5,7},{8,10},{9,11},{12,14},{13,15},{16,18},{17,... | collective-permute-start | bytes 12296 | tf_op jit(solution)/shard_map/ppermute | solution.py:37
  242.0 10.4 %collective-permute-start.19 = (f32[4,1,1,4,8,8]{5,3,0,4,2,1:T(4,128)S(1)}, f32[4,1,1,4,8,8]{5,3,0,4,2,1:T(4,128)S(1)}, u32[]{:S(2)}, u32[]{:S(2)}) collective-permute-start(f32[4,1,1,4,8,8]{5,3,0,4,2,1:T(4,128)S(1)} %bitcast.465), channel_id=1, source_target_pairs={{4,0},{8,4},{12,8},{16,12},{20,16},{24,20},{28,24},{5,1},{9,5},{13... | collective-permute-start | bytes 12296 | tf_op jit(solution)/shard_map/ppermute | solution.py:39
  245.5 6.4 %collective-permute-start.18 = (f32[4,1,1,4,8,8]{5,3,0,4,2,1:T(4,128)S(1)}, f32[4,1,1,4,8,8]{5,3,0,4,2,1:T(4,128)S(1)}, u32[]{:S(2)}, u32[]{:S(2)}) collective-permute-start(f32[4,1,1,4,8,8]{5,3,0,4,2,1:T(4,128)S(1)} %bitcast.466), channel_id=1, source_target_pairs={{0,4},{4,8},{8,12},{12,16},{16,20},{20,24},{24,28},{1,5},{5,9},{9,... | collective-permute-start | bytes 12296 | tf_op jit(solution)/shard_map/ppermute | solution.py:37
  (5 other events, 50.2 us)
where the time goes:
time: 272 us; the launch traced here: 267 us
  local copies, waits for them, and re-layouts  123 us (45%)
  starting transfers between devices  73.8 us (27%)
  other arithmetic  38.2 us (14%)
  matrix products  15.9 us (6%)
  waiting for transfers between devices  14.1 us (5%)
    ppermute x12, starting transfers between devices, extended(): lax.ppermute(tail, axis, [(i, (i + 1) % count) for i in range(ends)])  45.3 us
    scatter-add x6, local copies, waits for them, and re-layouts, tendency(): result.at[leading + (7,)]  31.4 us
    ppermute x12, starting transfers between devices, extended(): lax.ppermute(head, axis, [((i + 1) % count, i) for i in range(ends)])  15.5 us
    unnamed x36, local copies, waits for them, and re-layouts  12.1 us
    another operation x18, local copies, waits for them, and re-layouts, tendency(): jnp.stack([-divergence, COUPLING * forcing[0] - grad_x, COUPLING * forcin...  10 us
    scatter-add x5, local copies, waits for them, and re-layouts, tendency(): result.at[leading + (0,)]  9.58 us
    mul x18, other arithmetic, face_correction(): result = -0.5 * difference  9.56 us
    another operation x5, local copies, waits for them, and re-layouts, tendency(): lower_face = jnp.take(nodal_view, 0, axis=node_axis)  8.18 us
  transfers between devices with their start and end apart: 26, of which 6 were waited for; matrix products, arithmetic and copies ran while one was open for 26% of the time, Pallas kernels for 0%

commit v1 on v0

v1 whole, which is shorter than its diff:
```python
import functools

import jax
import jax.numpy as jnp
import numpy as np
from jax import lax
from jax.experimental import pallas as pl
from jax.experimental.pallas import tpu as pltpu
from jax.sharding import PartitionSpec as P

MESH = pl.DeviceIdType.MESH
SUB = 16
NODES = 512
LANES = 128
TILES = NODES // LANES
BLOCK = 8
GLL_POINTS = np.array(
    [
        -1.0,
        -0.8717401485096066,
        -0.5917001814331423,
        -0.2092992179024789,
        0.2092992179024789,
        0.5917001814331423,
        0.8717401485096066,
        1.0,
    ]
)
HALF_LIFT = 14.0
TIME_STEP = 0.01
COUPLING = 4.0
MOMENT_WEIGHT = 0.0625


def derivative_matrix():
    points = GLL_POINTS
    barycentric = np.ones(8)
    for j in range(8):
        for m in range(8):
            if m != j:
                barycentric[j] = barycentric[j] / (points[j] - points[m])
    matrix = np.zeros((8, 8))
    for i in range(8):
        for j in range(8):
            if i != j:
                matrix[i, j] = barycentric[j] / barycentric[i] / (points[i] - points[j])
        matrix[i, i] = -np.sum(matrix[i])
    return matrix


def basis_values():
    points = GLL_POINTS
    centres = -1.0 + (2.0 * np.arange(SUB) + 1.0) / SUB
    values = np.ones((SUB, 8))
    for j in range(8):
        for m in range(8):
            if m != j:
                values[:, j] = values[:, j] * (centres - points[m]) / (points[j] - points[m])
    return values


def constant_table():
    along = -derivative_matrix()
    along[0, 0] -= HALF_LIFT
    along[7, 7] += HALF_LIFT
    table = np.zeros((168, 2 * LANES))
    table[:128, :128] = np.kron(np.eye(2), np.kron(along, np.eye(8))).T
    table[:128, 128:] = np.kron(np.eye(16), along).T
    for j in range(TILES):
        for i in range(TILES):
            for h in range(2):
                lanes = slice(64 * h, 64 * h + 64)
                table[128 + 8 * j + 2 * i, lanes] = along[2 * j + h, 2 * i + h]
                table[129 + 8 * j + 2 * i, lanes] = along[2 * j + h, 2 * i + 1 - h]
    table[160:168, :SUB] = basis_values().T
    return table.astype(np.float32)


def each(count, body):
    if count <= 16:
        for k in range(count):
            body(k)
    else:
        lax.fori_loop(0, count, lambda k, c: (body(k), c)[1], 0)


def kernel(
    n,
    vel_ref, visc_ref, own_ref, elem_ref, pos_ref, state_ref, table_ref,
    mom_ref, next_ref,
    vel_in, state0, state1, state2, left_in, right_in, y_in, z_in,
    nodes, part, psend, precv,
    vel_send_sem, vel_recv_sem, face_send_sem, face_recv_sem, part_send_sem, part_recv_sem,
):
    f32 = jnp.float32
    gx, gy, gz = lax.axis_index("gx"), lax.axis_index("gy"), lax.axis_index("gz")
    last = n - 1
    has_left, has_right = gx > 0, gx < last
    low_y, low_z = gy == 0, gz == 0
    left = {"gx": jnp.maximum(gx - 1, 0)}
    right = {"gx": jnp.minimum(gx + 1, last)}
    other_y, other_z = {"gy": 1 - gy}, {"gz": 1 - gz}

    def peer(k):
        return lax.rem(gx + 1 + k, n)

    barrier = pltpu.get_barrier_semaphore()
    each(last, lambda k: pl.semaphore_signal(barrier, inc=1, device_id={"gx": peer(k)}, device_id_type=MESH))
    pl.semaphore_signal(barrier, inc=1, device_id=other_y, device_id_type=MESH)
    pl.semaphore_signal(barrier, inc=1, device_id=other_z, device_id_type=MESH)
    for c in range(4):
        state0[4 * c:4 * c + 4, :] = state_ref[c]
    pl.semaphore_wait(barrier, last + 2)

    def remote(src, dst, send_sem, recv_sem, device):
        return pltpu.make_async_remote_copy(
            src_ref=src, dst_ref=dst, send_sem=send_sem, recv_sem=recv_sem, device_id=device, device_id_type=MESH
        )

    def vel_copy(slot, device):
        return remote(vel_ref, vel_in.at[slot], vel_send_sem.at[slot], vel_recv_sem.at[slot], device)

    to_right, to_left = vel_copy(0, right), vel_copy(1, left)
    vel_y, vel_z = vel_copy(2, other_y), vel_copy(3, other_z)

    @pl.when(has_right)
    def _():
        to_right.start()

    @pl.when(has_left)
    def _():
        to_left.start()

    vel_z.start()
    vel_y.start()

    def faces(stage, state):
        ssem, rsem = face_send_sem.at[stage], face_recv_sem.at[stage]
        return (
            remote(state.at[:, NODES - LANES:], left_in.at[stage], ssem.at[0], rsem.at[0], right),
            remote(state.at[:, :LANES], right_in.at[stage], ssem.at[1], rsem.at[1], left),
            remote(state, y_in.at[stage], ssem.at[2], rsem.at[2], other_y),
            remote(state, z_in.at[stage], ssem.at[3], rsem.at[3], other_z),
        )

    def start_faces(copies):
        @pl.when(has_right)
        def _():
            copies[0].start()

        @pl.when(has_left)
        def _():
            copies[1].start()

        copies[3].start()
        copies[2].start()

    def wait_recv(copies):
        @pl.when(has_left)
        def _():
            copies[0].wait_recv()

        @pl.when(has_right)
        def _():
            copies[1].wait_recv()

        copies[2].wait_recv()
        copies[3].wait_recv()

    def wait_send(copies):
        @pl.when(has_right)
        def _():
            copies[0].wait_send()

        @pl.when(has_left)
        def _():
            copies[1].wait_send()

        copies[2].wait_send()
        copies[3].wait_send()

    faces0 = faces(0, state0)
    start_faces(faces0)

    basis = table_ref[160:168, :LANES]

    def weights(step, carry):
        for half in range(2):
            row = 2 * step + half
            position = jnp.broadcast_to(pos_ref[pl.ds(row, 1), :], (8, LANES))
            along = [
                jnp.take_along_axis(basis, index, axis=1, mode="promise_in_bounds")
                for index in (position >> 8, (position >> 4) & 15, position & 15)
            ]
            pair = along[0][:, None, :] * along[1][None, :, :]
            values = pair[:, :, None, :] * along[2][None, None, :, :]
            columns = pl.ds(pl.multiple_of(row * LANES, LANES), LANES)
            nodes[:, columns] = values.reshape(NODES, LANES).astype(jnp.bfloat16)
        return carry

    lax.fori_loop(0, 8, weights, 0)

    wait_recv((to_right, to_left, vel_y, vel_z))
    row_id = lax.broadcasted_iota(jnp.int32, (8, LANES), 0)
    lane_id = lax.broadcasted_iota(jnp.int32, (8, LANES), 1)
    sources = [[None, None] for _ in range(3)]
    own_vel = [[vel_ref[c, x].astype(f32) for x in range(2)] for c in range(3)]
    from_left = [jnp.where(has_left, vel_in[0, c, 1].astype(f32), 0.0) for c in range(3)]
    from_right = [jnp.where(has_right, vel_in[1, c, 0].astype(f32), 0.0) for c in range(3)]
    for x in range(2):
        grads, laplace = [], []
        for c in range(3):
            centre = own_vel[c][x]
            beside_y, beside_z = vel_in[2, c, x].astype(f32), vel_in[3, c, x].astype(f32)
            plus_x = own_vel[c][1] if x == 0 else from_right[c]
            minus_x = from_left[c] if x == 0 else own_vel[c][0]
            plus_y = pltpu.roll(jnp.where(row_id == 0, jnp.where(low_y, beside_y, 0.0), centre), 7, 0)
            minus_y = pltpu.roll(jnp.where(row_id == 7, jnp.where(low_y, 0.0, beside_y), centre), 1, 0)
            plus_z = pltpu.roll(jnp.where(lane_id == 0, jnp.where(low_z, beside_z, 0.0), centre), LANES - 1, 1)
            minus_z = pltpu.roll(jnp.where(lane_id == LANES - 1, jnp.where(low_z, 0.0, beside_z), centre), 1, 1)
            grads.append((0.5 * (plus_x - minus_x), 0.5 * (plus_y - minus_y), 0.5 * (plus_z - minus_z)))
            laplace.append(plus_x + minus_x + plus_y + minus_y + plus_z + minus_z - 6.0 * centre)
        curl = (
            grads[2][1] - grads[1][2],
            grads[0][2] - grads[2][0],
            grads[1][0] - grads[0][1],
        )
        for c in range(3):
            d, e = (c + 1) % 3, (c + 2) % 3
            lamb = curl[d] * own_vel[e][x] - curl[e] * own_vel[d][x]
            value = visc_ref[x] * laplace[c] - lamb
            sources[c][x] = value.astype(jnp.bfloat16).astype(f32)

    rows16 = lax.broadcasted_iota(jnp.int32, (16, LANES), 0)
    block = min(BLOCK, n)
    owner_id = lax.broadcasted_iota(jnp.int32, (block, 16, LANES), 0) * 4

    def project(first):
        pieces = []
        for x in range(2):
            for y in range(8):
                row = 8 * x + y
                segment = own_ref[row:row + 1, :] * 4 + elem_ref[row:row + 1, :] - 4 * first
                segment = jnp.broadcast_to(segment, (16, LANES)) - (rows16 & 3)
                s = [jnp.broadcast_to(sources[c][x][y:y + 1, :], (16, LANES)) for c in range(3)]
                value = jnp.where(rows16 < 4, 0.0, jnp.where(rows16 < 8, s[0], jnp.where(rows16 < 12, s[1], s[2])))
                piece = jnp.where(segment[None] == owner_id, value[None], 0.0)
                pieces.append(piece.reshape(block * 16, LANES).astype(jnp.bfloat16))
        weighted = jnp.concatenate(pieces, axis=1)
        total = lax.dot_general(
            weighted, nodes[...], (((1,), (1,)), ((), ())), preferred_element_type=f32
        ).reshape(block, 16, NODES) * MOMENT_WEIGHT
        part[pl.ds(first, block)] = total
        psend[pl.ds(first, block)] = total.astype(jnp.bfloat16)

    if n == block:
        project(0)
    else:
        lax.fori_loop(0, n // block, lambda k, c: (project(k * block), c)[1], 0)

    def part_out(k):
        to = peer(k)
        return remote(psend.at[to], precv.at[gx], part_send_sem.at[to], part_recv_sem.at[gx], {"gx": to})

    def part_into(k):
        by = peer(k)
        return remote(psend.at[by], precv.at[by], part_send_sem.at[by], part_recv_sem.at[by], {"gx": by})

    each(last, lambda k: part_out(k).start())

    lane16 = lax.broadcasted_iota(jnp.int32, (16, LANES), 1)
    b_id, c_id, e_id = (lane16 >> 3) & 7, lane16 & 7, rows16 & 3
    b_low, b_high, c_low, c_high = b_id == 0, b_id == 7, c_id == 0, c_id == 7
    on_bc = (b_low | b_high).astype(f32) + (c_low | c_high).astype(f32)
    first_half = lane16 < 64

    def tiles_of(ref):
        return [ref[:, LANES * j:LANES * (j + 1)] for j in range(TILES)]

    def local_part(x):
        top = [t[:8] for t in x]
        swapped = [pltpu.roll(t, 64, 1) for t in top]
        both = jnp.concatenate(x, axis=0)
        within = jnp.dot(
            both, table_ref[:128, :], precision=lax.Precision.HIGHEST, preferred_element_type=f32
        )
        result = []
        for j in range(TILES):
            along_a = None
            for i in range(TILES):
                at = 128 + 8 * j + 2 * i
                term = table_ref[at:at + 1, :LANES] * top[i] + table_ref[at + 1:at + 2, :LANES] * swapped[i]
                along_a = term if along_a is None else along_a + term
            faces_here = on_bc
            if j == 0:
                faces_here = on_bc + first_half.astype(f32)
            if j == TILES - 1:
                faces_here = on_bc + 1.0 - first_half.astype(f32)
            along_b = within[16 * j:16 * j + 16, :LANES]
            along_c = within[16 * j:16 * j + 16, LANES:]
            result.append((along_a, along_b, along_c, -faces_here * x[j]))
        return result

    def tendency(x, local, stage):
        result = []
        for j in range(TILES):
            columns = slice(LANES * j, LANES * (j + 1))
            along_a, along_b, along_c, faces_here = local[j]
            beside_y, beside_z = y_in[stage, :, columns], z_in[stage, :, columns]
            shifted = pltpu.roll(beside_y, jnp.where(low_y, 56, 72), 1)
            outer_b = jnp.where(jnp.where(low_y, b_id, 7 - b_id) == 7, shifted, 0.0)
            signed_b = jnp.where(low_y, outer_b, -outer_b)
            above = jnp.where(e_id == 3, jnp.where(low_z, pltpu.roll(beside_z, 3, 0), 0.0), pltpu.roll(x[j], 15, 0))
            below = jnp.where(e_id == 0, jnp.where(low_z, 0.0, pltpu.roll(beside_z, 13, 0)), pltpu.roll(x[j], 1, 0))
            upper = jnp.where(c_high, pltpu.roll(above, 7, 1), 0.0)
            lower = jnp.where(c_low, pltpu.roll(below, LANES - 7, 1), 0.0)
            outer = outer_b + upper + lower + faces_here
            if j == 0:
                outer_a = jnp.where(first_half & has_left, pltpu.roll(left_in[stage], 64, 1), 0.0)
                along_a, outer = along_a + HALF_LIFT * outer_a[:8], outer + outer_a
            if j == TILES - 1:
                outer_a = jnp.where(~first_half & has_right, pltpu.roll(right_in[stage], 64, 1), 0.0)
                along_a, outer = along_a - HALF_LIFT * outer_a[:8], outer + outer_a
            along_b = along_b - HALF_LIFT * signed_b
            along_c = along_c - HALF_LIFT * (upper - lower)
            swapped = jnp.concatenate(
                [along_a[4:8] + along_b[8:12] + along_c[12:16], along_a[0:4], along_b[0:4], along_c[0:4]], axis=0
            )
            result.append(swapped + HALF_LIFT * outer)
        return result

    start = tiles_of(state0)
    local = local_part(start)
    wait_recv(faces0)
    change = tendency(start, local, 0)
    early = [start[j] + TIME_STEP * change[j] for j in range(TILES)]

    each(last, lambda k: part_into(k).wait_recv())
    forcing = part[pl.ds(gx, 1)][0]
    if n <= 16:
        for k in range(last):
            forcing = forcing + precv[pl.ds(peer(k), 1)][0].astype(f32)
    else:
        forcing = lax.fori_loop(
            0, last, lambda k, total: total + precv[pl.ds(peer(k), 1)][0].astype(f32), forcing
        )
    push = [COUPLING * forcing[:, LANES * j:LANES * (j + 1)] for j in range(TILES)]

    one = [early[j] + TIME_STEP * push[j] for j in range(TILES)]
    for j in range(TILES):
        state1[:, LANES * j:LANES * (j + 1)] = one[j]
    faces1 = faces(1, state1)
    start_faces(faces1)
    for m in range(3):
        for e in range(4):
            mom_ref[0, 0, e, m:m + 1, :] = forcing[4 * m + 4 + e:4 * m + 5 + e, :]
    local = local_part(one)
    wait_recv(faces1)
    change = tendency(one, local, 1)
    two = [
        0.75 * start[j] + 0.25 * (one[j] + TIME_STEP * (change[j] + push[j])) for j in range(TILES)
    ]
    for j in range(TILES):
        state2[:, LANES * j:LANES * (j + 1)] = two[j]
    faces2 = faces(2, state2)
    start_faces(faces2)
    local = local_part(two)
    wait_recv(faces2)
    change = tendency(two, local, 2)
    for j in range(TILES):
        final = (1.0 / 3.0) * start[j] + (2.0 / 3.0) * (two[j] + TIME_STEP * (change[j] + push[j]))
        for c in range(4):
            next_ref[c, 0, 0, :, LANES * j:LANES * (j + 1)] = final[4 * c:4 * c + 4]

    wait_send((to_right, to_left, vel_y, vel_z))
    wait_send(faces0)
    wait_send(faces1)
    wait_send(faces2)
    each(last, lambda k: part_out(k).wait_send())


def solution(mesh):
    n = mesh.shape["gx"]
    assert mesh.shape["gy"] == 2 and mesh.shape["gz"] == 2
    f32, bf16 = jnp.float32, jnp.bfloat16
    dma = pltpu.SemaphoreType.DMA
    vmem = pl.BlockSpec(memory_space=pltpu.VMEM)

    def on_device(velocity, eddy_viscosity, cell_owner, cell_element, cell_position, acoustic_state):
        call = pl.pallas_call(
            functools.partial(kernel, n),
            out_shape=(
                jax.ShapeDtypeStruct((1, 1, 4, 3, NODES), f32),
                jax.ShapeDtypeStruct((4, 1, 1, 4, NODES), f32),
            ),
            in_specs=[vmem] * 7,
            out_specs=(vmem, vmem),
            scratch_shapes=[
                pltpu.VMEM((4, 3, 2, 8, LANES), bf16),
                pltpu.VMEM((16, NODES), f32),
                pltpu.VMEM((16, NODES), f32),
                pltpu.VMEM((16, NODES), f32),
                pltpu.VMEM((3, 16, LANES), f32),
                pltpu.VMEM((3, 16, LANES), f32),
                pltpu.VMEM((3, 16, NODES), f32),
                pltpu.VMEM((3, 16, NODES), f32),
                pltpu.VMEM((NODES, 16 * LANES), bf16),
                pltpu.VMEM((n, 16, NODES), f32),
                pltpu.VMEM((n, 16, NODES), bf16),
                pltpu.VMEM((n, 16, NODES), bf16),
                dma((4,)),
                dma((4,)),
                dma((3, 4)),
                dma((3, 4)),
                dma((n,)),
                dma((n,)),
            ],
            compiler_params=pltpu.CompilerParams(
                collective_id=0, has_side_effects=True, vmem_limit_bytes=40 * 1024 * 1024
            ),
        )
        return call(
            velocity,
            eddy_viscosity,
            cell_owner.reshape(16, LANES),
            cell_element.reshape(16, LANES),
            cell_position.reshape(16, LANES),
            acoustic_state.reshape(4, 4, NODES),
            jnp.asarray(constant_table()),
        )

    in_specs = (
        P(None, "gx", "gy", "gz"),
        P("gx", "gy", "gz"),
        P("gy", "gz", "gx", None),
        P("gy", "gz", "gx"),
        P("gy", "gz", "gx"),
        P(None, "gx", "gy", "gz", None),
    )
    out_specs = (P("gx", "gy", "gz", None, None), P(None, "gx", "gy", "gz", None))
    return jax.shard_map(on_device, mesh=mesh, in_specs=in_specs, out_specs=out_specs, check_vma=False)
```

time: 272 us -> 27.9 us (0.10); the launches traced: 267 us -> 27.5 us
  local copies, waits for them, and re-layouts: 123 us -> 6.4 us
  starting transfers between devices: 73.8 us -> 0 us
  other arithmetic: 38.2 us -> 0 us
  Pallas kernels: 0 us -> 20.4 us
  matrix products: 15.9 us -> 0 us
  waiting for transfers between devices: 14.1 us -> 0 us
    ppermute x24 -> x0, starting transfers between devices: 60.8 us -> none  [the longest x12 45.3 us: extended(): lax.ppermute(tail, axis, [(i, (i + 1) % count) for i in range(ends)])]
    scatter-add x12 -> x0, local copies, waits for them, and re-layouts: 41.1 us -> none  [the longest x6 31.4 us: tendency(): result.at[leading + (7,)]]
    another operation x33 -> x0, local copies, waits for them, and re-layouts: 30.7 us -> none  [the longest x18 10 us: tendency(): jnp.stack([-divergence, COUPLING * forcing[0] - grad_x, COUPLING * forcin...]
    pallas_call x0 -> x1, Pallas kernels: none -> 20.4 us  [on_device(): call(velocity, eddy_viscosity, cell_owner.reshape(16, LANES), cell_elemen...]
    dot_general x22 -> x0, matrix products: 15.9 us -> none  [the longest x3 3.1 us: tendency(): grad_x = jnp.dot(pressure, tables[0], precision=highest)]
    mul x26 -> x0, other arithmetic: 14.3 us -> none  [the longest x18 9.56 us: face_correction(): result = -0.5 * difference]
    scatter x2 -> x0, local copies, waits for them, and re-layouts: 13.8 us -> none  [the longest x1 7.02 us: on_device(): send_source = jnp.zeros((3, owner_count * capacity), jnp.bfloat16).at[:,...]
    all_to_all x2 -> x0, starting transfers between devices: 13 us -> none  [the longest x1 6.62 us: on_device(): lax.all_to_all(send_source, 'gx', split_axis=1, concat_axis=1, tiled=True)]
  transfers between devices with their start and end apart: 26 -> 0, of which waited for: 6 -> 0; matrix products, arithmetic and copies ran while one was open for 26% -> 0% of each run, Pallas kernels for 0% -> 0%
where the time goes in v1:
time: 27.9 us; the launch traced here: 27.5 us
  Pallas kernels  20.4 us (73%)
  local copies, waits for them, and re-layouts  6.4 us (23%)
  between operations  0.65 us (2%)
    pallas_call x1, Pallas kernels, on_device(): call(velocity, eddy_viscosity, cell_owner.reshape(16, LANES), cell_elemen...  20.4 us
    unnamed x15, local copies, waits for them, and re-layouts  5.78 us
    pallas_call x1, local copies, waits for them, and re-layouts, on_device(): call(velocity, eddy_viscosity, cell_owner.reshape(16, LANES), cell_elemen...  0.62 us

profile of v1, /device:TPU:0, one launch (start us, length us, event | category | flops | bytes accessed | tf_op | source)
XLA Modules:
  0.0 27.5 jit_solution(12263459894640375609)
XLA Ops:
  0.6 0.0 copy-start
  0.6 0.9 %copy-done = f32[168,256]{1,0:T(8,128)S(1)} copy-done((f32[168,256]{1,0:T(8,128)S(1)}, f32[168,256]{1,0:T(8,128)}, u32[]{:S(2)}) %copy-start) | copy-done | bytes 172056
  1.6 0.0 copy-start.1
  1.6 0.8 %copy-done.1 = f32[4,1,1,4,512]{4,3,2,1,0:T(4,128)S(1)} copy-done((f32[4,1,1,4,512]{4,3,2,1,0:T(4,128)S(1)}, f32[4,1,1,4,512]{4,3,2,1,0:T(4,128)}, u32[]{:S(2)}) %copy-start.1) | copy-done | bytes 32792
  2.3 0.0 copy-start.2
  2.3 0.7 %copy-done.2 = bf16[3,2,8,128]{3,2,1,0:T(8,128)(2,1)S(1)} copy-done((bf16[3,2,8,128]{3,2,1,0:T(8,128)(2,1)S(1)}, bf16[3,2,8,128]{3,2,1,0:T(8,128)(2,1)}, u32[]{:S(2)}) %copy-start.2) | copy-done | bytes 12312
  3.0 0.0 copy-start.3
  3.0 0.7 %copy-done.3 = f32[2,8,128]{2,1,0:T(8,128)S(1)} copy-done((f32[2,8,128]{2,1,0:T(8,128)S(1)}, f32[2,8,128]{2,1,0:T(8,128)}, u32[]{:S(2)}) %copy-start.3) | copy-done | bytes 8216
  3.7 0.0 copy-start.4
  3.7 0.7 %copy-done.4 = s32[1,1,2048,1]{2,3,1,0:T(1,128)S(1)} copy-done((s32[1,1,2048,1]{2,3,1,0:T(1,128)S(1)}, s32[1,1,2048,1]{2,3,1,0:T(1,128)}, u32[]{:S(2)}) %copy-start.4) | copy-done | bytes 8216
  4.4 0.0 copy-start.5
  4.4 0.7 %copy-done.5 = s32[1,1,2048]{2,1,0:T(1,128)S(1)} copy-done((s32[1,1,2048]{2,1,0:T(1,128)S(1)}, s32[1,1,2048]{2,1,0:T(1,128)}, u32[]{:S(2)}) %copy-start.5) | copy-done | bytes 8216
  5.1 0.0 copy-start.6
  5.1 0.7 %copy-done.6 = s32[1,1,2048]{2,1,0:T(1,128)S(1)} copy-done((s32[1,1,2048]{2,1,0:T(1,128)S(1)}, s32[1,1,2048]{2,1,0:T(1,128)}, u32[]{:S(2)}) %copy-start.6) | copy-done | bytes 8216
  5.8 20.4 %shard_map.86 = (f32[1,1,4,3,512]{4,3,2,1,0:T(4,128)S(1)}, f32[4,1,1,4,512]{4,3,2,1,0:T(4,128)S(1)}) custom-call(bf16[3,2,8,128]{3,2,1,0:T(8,128)(2,1)S(1)} %copy-done.2, f32[2,8,128]{2,1,0:T(8,128)S(1)} %copy-done.3, s32[16,128]{1,0:T(8,128)S(1)} %bitcast.5, s32[16,128]{1,0:T(8,128)S(1)} %bitcast.6, s32[16,128]{1,0:T(8,128)S(1)} %bitcast.7, ...), custom_call_target="tpu_custom_call" | custom-call | tf_op jit(solution)/shard_map/pallas_call | solution.py:422
  26.2 0.6 %copy.9 = f32[1,1,4,3,512]{4,2,3,1,0:T(4,128)} copy(f32[1,1,4,3,512]{4,3,2,1,0:T(4,128)S(1)} %get-tuple-element.2) | data formatting | bytes 49152 | tf_op jit(solution)/shard_map/pallas_call | solution.py:422
  26.8 0.6 %copy.11 = f32[4,1,1,4,512]{4,3,2,1,0:T(4,128)} copy(f32[4,1,1,4,512]{4,3,2,1,0:T(4,128)S(1)} %get-tuple-element.7) | data formatting | bytes 65536
Async XLA Ops:
  0.6 0.9 %copy-start = (f32[168,256]{1,0:T(8,128)S(1)}, f32[168,256]{1,0:T(8,128)}, u32[]{:S(2)}) copy-start(f32[168,256]{1,0:T(8,128)} %constant.2.clone.table_ref) | copy-start | bytes 516100
  1.6 0.8 %copy-start.1 = (f32[4,1,1,4,512]{4,3,2,1,0:T(4,128)S(1)}, f32[4,1,1,4,512]{4,3,2,1,0:T(4,128)}, u32[]{:S(2)}) copy-start(f32[4,1,1,4,512]{4,3,2,1,0:T(4,128)} %param.12) | copy-start | bytes 98308
  2.3 0.7 %copy-start.2 = (bf16[3,2,8,128]{3,2,1,0:T(8,128)(2,1)S(1)}, bf16[3,2,8,128]{3,2,1,0:T(8,128)(2,1)}, u32[]{:S(2)}) copy-start(bf16[3,2,8,128]{3,2,1,0:T(8,128)(2,1)} %vel_ref.1) | copy-start | bytes 36868
  3.0 0.7 %copy-start.3 = (f32[2,8,128]{2,1,0:T(8,128)S(1)}, f32[2,8,128]{2,1,0:T(8,128)}, u32[]{:S(2)}) copy-start(f32[2,8,128]{2,1,0:T(8,128)} %visc_ref.1) | copy-start | bytes 24580
  3.7 0.7 %copy-start.4 = (s32[1,1,2048,1]{2,3,1,0:T(1,128)S(1)}, s32[1,1,2048,1]{2,3,1,0:T(1,128)}, u32[]{:S(2)}) copy-start(s32[1,1,2048,1]{2,3,1,0:T(1,128)} %param.9) | copy-start | bytes 24580
  4.4 0.7 %copy-start.5 = (s32[1,1,2048]{2,1,0:T(1,128)S(1)}, s32[1,1,2048]{2,1,0:T(1,128)}, u32[]{:S(2)}) copy-start(s32[1,1,2048]{2,1,0:T(1,128)} %param.10) | copy-start | bytes 24580
  5.1 0.7 %copy-start.6 = (s32[1,1,2048]{2,1,0:T(1,128)S(1)}, s32[1,1,2048]{2,1,0:T(1,128)}, u32[]{:S(2)}) copy-start(s32[1,1,2048]{2,1,0:T(1,128)} %param.11) | copy-start | bytes 24580

commit v2 on v1

--- a/solution.py
+++ b/solution.py
@@ -86,8 +86,9 @@
 
 def kernel(
     n,
-    vel_ref, visc_ref, own_ref, elem_ref, pos_ref, state_ref, table_ref,
-    mom_ref, next_ref,
+    vel_hbm, visc_hbm, own_hbm, elem_hbm, pos_hbm, state_hbm, table_hbm,
+    out_ref,
+    vel_ref, visc_ref, own_ref, elem_ref, pos_ref, state_ref, table_ref, load_sem, z_out,
     vel_in, state0, state1, state2, left_in, right_in, y_in, z_in,
     nodes, part, psend, precv,
     vel_send_sem, vel_recv_sem, face_send_sem, face_recv_sem, part_send_sem, part_recv_sem,
@@ -108,8 +109,17 @@
     each(last, lambda k: pl.semaphore_signal(barrier, inc=1, device_id={"gx": peer(k)}, device_id_type=MESH))
     pl.semaphore_signal(barrier, inc=1, device_id=other_y, device_id_type=MESH)
     pl.semaphore_signal(barrier, inc=1, device_id=other_z, device_id_type=MESH)
-    for c in range(4):
-        state0[4 * c:4 * c + 4, :] = state_ref[c]
+    loads = [
+        pltpu.make_async_copy(src, dst, load_sem.at[k])
+        for k, (src, dst) in enumerate(
+            (
+                (vel_hbm, vel_ref), (pos_hbm, pos_ref), (table_hbm, table_ref), (state_hbm, state_ref),
+                (own_hbm, own_ref), (elem_hbm, elem_ref), (visc_hbm, visc_ref),
+            )
+        )
+    ]
+    for load in loads:
+        load.start()
     pl.semaphore_wait(barrier, last + 2)
 
     def remote(src, dst, send_sem, recv_sem, device):
@@ -118,7 +128,7 @@
         )
 
     def vel_copy(slot, device):
-        return remote(vel_ref, vel_in.at[slot], vel_send_sem.at[slot], vel_recv_sem.at[slot], device)
+        return remote(vel_hbm, vel_in.at[slot], vel_send_sem.at[slot], vel_recv_sem.at[slot], device)
 
     to_right, to_left = vel_copy(0, right), vel_copy(1, left)
     vel_y, vel_z = vel_copy(2, other_y), vel_copy(3, other_z)
@@ -140,7 +150,7 @@
             remote(state.at[:, NODES - LANES:], left_in.at[stage], ssem.at[0], rsem.at[0], right),
             remote(state.at[:, :LANES], right_in.at[stage], ssem.at[1], rsem.at[1], left),
             remote(state, y_in.at[stage], ssem.at[2], rsem.at[2], other_y),
-            remote(state, z_in.at[stage], ssem.at[3], rsem.at[3], other_z),
+            remote(z_out.at[stage], z_in.at[stage], ssem.at[3], rsem.at[3], other_z),
         )
 
     def start_faces(copies):
@@ -179,8 +189,31 @@
         copies[2].wait_send()
         copies[3].wait_send()
 
+    row_id = lax.broadcasted_iota(jnp.int32, (8, LANES), 0)
+    lane_id = lax.broadcasted_iota(jnp.int32, (8, LANES), 1)
+    rows16 = lax.broadcasted_iota(jnp.int32, (16, LANES), 0)
+    lane16 = lax.broadcasted_iota(jnp.int32, (16, LANES), 1)
+    b_id, c_id, e_id = (lane16 >> 3) & 7, lane16 & 7, rows16 & 3
+
+    def tiles_of(ref):
+        return [ref[:, LANES * j:LANES * (j + 1)] for j in range(TILES)]
+
+    def pack_z(x, stage):
+        packed = x[0]
+        for j in range(TILES):
+            shift = jnp.where(low_z, (j - 7) % LANES, j)
+            packed = jnp.where(c_id == j, pltpu.roll(x[j], shift, 1), packed)
+        z_out[stage] = packed
+
+    loads[3].wait()
+    for c in range(4):
+        state0[4 * c:4 * c + 4, :] = state_ref[c]
+    start = tiles_of(state0)
+    pack_z(start, 0)
     faces0 = faces(0, state0)
     start_faces(faces0)
+    loads[1].wait()
+    loads[2].wait()
 
     basis = table_ref[160:168, :LANES]
 
@@ -200,9 +233,10 @@
 
     lax.fori_loop(0, 8, weights, 0)
 
+    loads[0].wait()
+    for load in loads[4:]:
+        load.wait()
     wait_recv((to_right, to_left, vel_y, vel_z))
-    row_id = lax.broadcasted_iota(jnp.int32, (8, LANES), 0)
-    lane_id = lax.broadcasted_iota(jnp.int32, (8, LANES), 1)
     sources = [[None, None] for _ in range(3)]
     own_vel = [[vel_ref[c, x].astype(f32) for x in range(2)] for c in range(3)]
     from_left = [jnp.where(has_left, vel_in[0, c, 1].astype(f32), 0.0) for c in range(3)]
@@ -231,7 +265,6 @@
             value = visc_ref[x] * laplace[c] - lamb
             sources[c][x] = value.astype(jnp.bfloat16).astype(f32)
 
-    rows16 = lax.broadcasted_iota(jnp.int32, (16, LANES), 0)
     block = min(BLOCK, n)
     owner_id = lax.broadcasted_iota(jnp.int32, (block, 16, LANES), 0) * 4
 
@@ -250,8 +283,17 @@
         total = lax.dot_general(
             weighted, nodes[...], (((1,), (1,)), ((), ())), preferred_element_type=f32
         ).reshape(block, 16, NODES) * MOMENT_WEIGHT
-        part[pl.ds(first, block)] = total
-        psend[pl.ds(first, block)] = total.astype(jnp.bfloat16)
+        packed = jnp.concatenate(
+            [
+                jnp.concatenate(
+                    [total[:, 4 * m + 4:4 * m + 8, LANES * j:LANES * (j + 1)] for j in range(TILES)], axis=1
+                )
+                for m in range(3)
+            ],
+            axis=2,
+        )
+        part[pl.ds(first, block)] = packed
+        psend[pl.ds(first, block)] = packed.astype(jnp.bfloat16)
 
     if n == block:
         project(0)
@@ -268,14 +310,10 @@
 
     each(last, lambda k: part_out(k).start())
 
-    lane16 = lax.broadcasted_iota(jnp.int32, (16, LANES), 1)
-    b_id, c_id, e_id = (lane16 >> 3) & 7, lane16 & 7, rows16 & 3
     b_low, b_high, c_low, c_high = b_id == 0, b_id == 7, c_id == 0, c_id == 7
     on_bc = (b_low | b_high).astype(f32) + (c_low | c_high).astype(f32)
     first_half = lane16 < 64
-
-    def tiles_of(ref):
-        return [ref[:, LANES * j:LANES * (j + 1)] for j in range(TILES)]
+    on_z = jnp.where(low_z, c_id + e_id, 10 - c_id - e_id) == 10
 
     def local_part(x):
         top = [t[:8] for t in x]
@@ -298,23 +336,26 @@
                 faces_here = on_bc + 1.0 - first_half.astype(f32)
             along_b = within[16 * j:16 * j + 16, :LANES]
             along_c = within[16 * j:16 * j + 16, LANES:]
-            result.append((along_a, along_b, along_c, -faces_here * x[j]))
+            above = jnp.where(e_id == 3, 0.0, pltpu.roll(x[j], 15, 0))
+            below = jnp.where(e_id == 0, 0.0, pltpu.roll(x[j], 1, 0))
+            upper = jnp.where(c_high, pltpu.roll(above, 7, 1), 0.0)
+            lower = jnp.where(c_low, pltpu.roll(below, LANES - 7, 1), 0.0)
+            along_c = along_c - HALF_LIFT * (upper - lower)
+            result.append((along_a, along_b, along_c, upper + lower - faces_here * x[j]))
         return result
 
-    def tendency(x, local, stage):
+    def tendency(local, stage):
         result = []
+        beside_z = pltpu.roll(z_in[stage], jnp.where(low_z, 3, 13), 0)
         for j in range(TILES):
             columns = slice(LANES * j, LANES * (j + 1))
             along_a, along_b, along_c, faces_here = local[j]
-            beside_y, beside_z = y_in[stage, :, columns], z_in[stage, :, columns]
+            beside_y = y_in[stage, :, columns]
             shifted = pltpu.roll(beside_y, jnp.where(low_y, 56, 72), 1)
             outer_b = jnp.where(jnp.where(low_y, b_id, 7 - b_id) == 7, shifted, 0.0)
             signed_b = jnp.where(low_y, outer_b, -outer_b)
-            above = jnp.where(e_id == 3, jnp.where(low_z, pltpu.roll(beside_z, 3, 0), 0.0), pltpu.roll(x[j], 15, 0))
-            below = jnp.where(e_id == 0, jnp.where(low_z, 0.0, pltpu.roll(beside_z, 13, 0)), pltpu.roll(x[j], 1, 0))
-            upper = jnp.where(c_high, pltpu.roll(above, 7, 1), 0.0)
-            lower = jnp.where(c_low, pltpu.roll(below, LANES - 7, 1), 0.0)
-            outer = outer_b + upper + lower + faces_here
+            outer_c = jnp.where(on_z, pltpu.roll(beside_z, jnp.where(low_z, 7 - j, (LANES - j) % LANES), 1), 0.0)
+            outer = outer_b + outer_c + faces_here
             if j == 0:
                 outer_a = jnp.where(first_half & has_left, pltpu.roll(left_in[stage], 64, 1), 0.0)
                 along_a, outer = along_a + HALF_LIFT * outer_a[:8], outer + outer_a
@@ -322,17 +363,16 @@
                 outer_a = jnp.where(~first_half & has_right, pltpu.roll(right_in[stage], 64, 1), 0.0)
                 along_a, outer = along_a - HALF_LIFT * outer_a[:8], outer + outer_a
             along_b = along_b - HALF_LIFT * signed_b
-            along_c = along_c - HALF_LIFT * (upper - lower)
+            along_c = along_c - HALF_LIFT * jnp.where(low_z, outer_c, -outer_c)
             swapped = jnp.concatenate(
                 [along_a[4:8] + along_b[8:12] + along_c[12:16], along_a[0:4], along_b[0:4], along_c[0:4]], axis=0
             )
             result.append(swapped + HALF_LIFT * outer)
         return result
 
-    start = tiles_of(state0)
     local = local_part(start)
     wait_recv(faces0)
-    change = tendency(start, local, 0)
+    change = tendency(local, 0)
     early = [start[j] + TIME_STEP * change[j] for j in range(TILES)]
 
     each(last, lambda k: part_into(k).wait_recv())
@@ -344,33 +384,39 @@
         forcing = lax.fori_loop(
             0, last, lambda k, total: total + precv[pl.ds(peer(k), 1)][0].astype(f32), forcing
         )
-    push = [COUPLING * forcing[:, LANES * j:LANES * (j + 1)] for j in range(TILES)]
+    moments = [
+        [forcing[4 * j:4 * j + 4, LANES * m:LANES * (m + 1)] for m in range(3)] for j in range(TILES)
+    ]
+    none = jnp.zeros((4, LANES), f32)
+    push = [COUPLING * jnp.concatenate([none] + moments[j], axis=0) for j in range(TILES)]
 
     one = [early[j] + TIME_STEP * push[j] for j in range(TILES)]
     for j in range(TILES):
         state1[:, LANES * j:LANES * (j + 1)] = one[j]
+    pack_z(one, 1)
     faces1 = faces(1, state1)
     start_faces(faces1)
     for m in range(3):
-        for e in range(4):
-            mom_ref[0, 0, e, m:m + 1, :] = forcing[4 * m + 4 + e:4 * m + 5 + e, :]
+        for j in range(TILES):
+            out_ref[4 + m, :, LANES * j:LANES * (j + 1)] = moments[j][m]
     local = local_part(one)
     wait_recv(faces1)
-    change = tendency(one, local, 1)
+    change = tendency(local, 1)
     two = [
         0.75 * start[j] + 0.25 * (one[j] + TIME_STEP * (change[j] + push[j])) for j in range(TILES)
     ]
     for j in range(TILES):
         state2[:, LANES * j:LANES * (j + 1)] = two[j]
+    pack_z(two, 2)
     faces2 = faces(2, state2)
     start_faces(faces2)
     local = local_part(two)
     wait_recv(faces2)
-    change = tendency(two, local, 2)
+    change = tendency(local, 2)
     for j in range(TILES):
         final = (1.0 / 3.0) * start[j] + (2.0 / 3.0) * (two[j] + TIME_STEP * (change[j] + push[j]))
         for c in range(4):
-            next_ref[c, 0, 0, :, LANES * j:LANES * (j + 1)] = final[4 * c:4 * c + 4]
+            out_ref[c, :, LANES * j:LANES * (j + 1)] = final[4 * c:4 * c + 4]
 
     wait_send((to_right, to_left, vel_y, vel_z))
     wait_send(faces0)
@@ -384,18 +430,23 @@
     assert mesh.shape["gy"] == 2 and mesh.shape["gz"] == 2
     f32, bf16 = jnp.float32, jnp.bfloat16
     dma = pltpu.SemaphoreType.DMA
-    vmem = pl.BlockSpec(memory_space=pltpu.VMEM)
 
     def on_device(velocity, eddy_viscosity, cell_owner, cell_element, cell_position, acoustic_state):
         call = pl.pallas_call(
             functools.partial(kernel, n),
-            out_shape=(
-                jax.ShapeDtypeStruct((1, 1, 4, 3, NODES), f32),
-                jax.ShapeDtypeStruct((4, 1, 1, 4, NODES), f32),
-            ),
-            in_specs=[vmem] * 7,
-            out_specs=(vmem, vmem),
+            out_shape=jax.ShapeDtypeStruct((7, 4, NODES), f32),
+            in_specs=[pl.BlockSpec(memory_space=pltpu.HBM)] * 7,
+            out_specs=pl.BlockSpec(memory_space=pltpu.VMEM),
             scratch_shapes=[
+                pltpu.VMEM((3, 2, 8, LANES), bf16),
+                pltpu.VMEM((2, 8, LANES), f32),
+                pltpu.VMEM((16, LANES), jnp.int32),
+                pltpu.VMEM((16, LANES), jnp.int32),
+                pltpu.VMEM((16, LANES), jnp.int32),
+                pltpu.VMEM((4, 4, NODES), f32),
+                pltpu.VMEM((168, 2 * LANES), f32),
+                dma((7,)),
+                pltpu.VMEM((3, 16, LANES), f32),
                 pltpu.VMEM((4, 3, 2, 8, LANES), bf16),
                 pltpu.VMEM((16, NODES), f32),
                 pltpu.VMEM((16, NODES), f32),
@@ -403,11 +454,11 @@
                 pltpu.VMEM((3, 16, LANES), f32),
                 pltpu.VMEM((3, 16, LANES), f32),
                 pltpu.VMEM((3, 16, NODES), f32),
-                pltpu.VMEM((3, 16, NODES), f32),
+                pltpu.VMEM((3, 16, LANES), f32),
                 pltpu.VMEM((NODES, 16 * LANES), bf16),
-                pltpu.VMEM((n, 16, NODES), f32),
-                pltpu.VMEM((n, 16, NODES), bf16),
-                pltpu.VMEM((n, 16, NODES), bf16),
+                pltpu.VMEM((n, 16, 3 * LANES), f32),
+                pltpu.VMEM((n, 16, 3 * LANES), bf16),
+                pltpu.VMEM((n, 16, 3 * LANES), bf16),
                 dma((4,)),
                 dma((4,)),
                 dma((3, 4)),
@@ -416,10 +467,10 @@
                 dma((n,)),
             ],
             compiler_params=pltpu.CompilerParams(
-                collective_id=0, has_side_effects=True, vmem_limit_bytes=40 * 1024 * 1024
+                collective_id=0, has_side_effects=True, vmem_limit_bytes=63 * 1024 * 1024
             ),
         )
-        return call(
+        out = call(
             velocity,
             eddy_viscosity,
             cell_owner.reshape(16, LANES),
@@ -428,6 +479,8 @@
             acoustic_state.reshape(4, 4, NODES),
             jnp.asarray(constant_table()),
         )
+        moments = jnp.transpose(out[4:], (1, 0, 2)).reshape(1, 1, 4, 3, NODES)
+        return moments, out[:4].reshape(4, 1, 1, 4, NODES)
 
     in_specs = (
         P(None, "gx", "gy", "gz"),

time: 27.9 us -> 24.7 us (0.89)
  local copies, waits for them, and re-layouts: 6.4 us -> 2.72 us
  Pallas kernels: 20.4 us -> 21.1 us
    unnamed x15 -> x1, local copies, waits for them, and re-layouts: 5.78 us -> 1.37 us
    reshape x0 -> x1, local copies, waits for them, and re-layouts: none -> 1.35 us  [on_device(): moments = jnp.transpose(out[4:], (1, 0, 2)).reshape(1, 1, 4, 3, NODES)]
    pallas_call x1, Pallas kernels: 20.4 us -> 21.1 us  [on_device(): call(velocity, eddy_viscosity, cell_owner.reshape(16, LANES), cell_elemen...]
    pallas_call x1 -> x0, local copies, waits for them, and re-layouts: 0.62 us -> none  [on_device(): call(velocity, eddy_viscosity, cell_owner.reshape(16, LANES), cell_elemen...]
where the time goes in v2:
time: 24.7 us; the launch traced here: 24.4 us
  Pallas kernels  21.1 us (85%)
  local copies, waits for them, and re-layouts  2.72 us (11%)
  between operations  0.64 us (3%)
    pallas_call x1, Pallas kernels, on_device(): call(velocity, eddy_viscosity, cell_owner.reshape(16, LANES), cell_elemen...  21.1 us
    unnamed x1, local copies, waits for them, and re-layouts  1.37 us
    reshape x1, local copies, waits for them, and re-layouts, on_device(): moments = jnp.transpose(out[4:], (1, 0, 2)).reshape(1, 1, 4, 3, NODES)  1.35 us

profile of v2, /device:TPU:0, one launch (start us, length us, event | category | flops | bytes accessed | tf_op | source)
XLA Modules:
  0.0 24.4 jit_solution(10118977942816240307)
XLA Ops:
  0.6 21.1 %shard_map.86 = f32[7,4,512]{2,1,0:T(4,128)} custom-call(bf16[3,2,8,128]{3,2,1,0:T(8,128)(2,1)} %vel_hbm.1, f32[2,8,128]{2,1,0:T(8,128)} %visc_hbm.1, s32[16,128]{1,0:T(8,128)} %bitcast.13, s32[16,128]{1,0:T(8,128)} %bitcast.14, s32[16,128]{1,0:T(8,128)} %bitcast.15, f32[4,4,512]{2,1,0:T(4,128)} %bitcast.12, f32[168,256]{1,0:T(8,128)} %constant.2.clone.table_hbm), custom_call_target="tpu_custom_call" | custom-call | tf_op jit(solution)/shard_map/pallas_call | solution.py:473
  21.7 1.3 %slice_bitcast_fusion.1 = f32[1,1,4,3,512]{4,2,3,1,0:T(4,128)} fusion(f32[7,4,512]{2,1,0:T(4,128)} %shard_map.86), kind=kLoop, calls=%fused_computation.1 | loop fusion | bytes 49152 | tf_op jit(solution)/shard_map/reshape | solution.py:482
  23.1 1.4 %slice_bitcast_fusion = f32[4,1,1,4,512]{4,3,2,1,0:T(4,128)} fusion(f32[7,4,512]{2,1,0:T(4,128)} %shard_map.86), kind=kLoop, calls=%fused_computation | loop fusion | bytes 65536

commit v3 on v2

--- a/solution.py
+++ b/solution.py
@@ -205,13 +205,6 @@
             packed = jnp.where(c_id == j, pltpu.roll(x[j], shift, 1), packed)
         z_out[stage] = packed
 
-    loads[3].wait()
-    for c in range(4):
-        state0[4 * c:4 * c + 4, :] = state_ref[c]
-    start = tiles_of(state0)
-    pack_z(start, 0)
-    faces0 = faces(0, state0)
-    start_faces(faces0)
     loads[1].wait()
     loads[2].wait()
 
@@ -233,6 +226,13 @@
 
     lax.fori_loop(0, 8, weights, 0)
 
+    loads[3].wait()
+    for c in range(4):
+        state0[4 * c:4 * c + 4, :] = state_ref[c]
+    start = tiles_of(state0)
+    pack_z(start, 0)
+    faces0 = faces(0, state0)
+    start_faces(faces0)
     loads[0].wait()
     for load in loads[4:]:
         load.wait()
@@ -434,7 +434,7 @@
     def on_device(velocity, eddy_viscosity, cell_owner, cell_element, cell_position, acoustic_state):
         call = pl.pallas_call(
             functools.partial(kernel, n),
-            out_shape=jax.ShapeDtypeStruct((7, 4, NODES), f32),
+            out_shape=pltpu.VMEM((7, 4, NODES), f32),
             in_specs=[pl.BlockSpec(memory_space=pltpu.HBM)] * 7,
             out_specs=pl.BlockSpec(memory_space=pltpu.VMEM),
             scratch_shapes=[

time: 24.7 us -> 22.5 us (0.911)
  local copies, waits for them, and re-layouts: 2.72 us -> 1.23 us
  Pallas kernels: 21.1 us -> 20.5 us
    unnamed x1, local copies, waits for them, and re-layouts: 1.37 us -> 0.62 us
    reshape x1, local copies, waits for them, and re-layouts: 1.35 us -> 0.61 us  [on_device(): moments = jnp.transpose(out[4:], (1, 0, 2)).reshape(1, 1, 4, 3, NODES)]
    pallas_call x1, Pallas kernels: 21.1 us -> 20.5 us  [on_device(): call(velocity, eddy_viscosity, cell_owner.reshape(16, LANES), cell_elemen...]
where the time goes in v3:
time: 22.5 us; the launch traced here: 22.3 us
  Pallas kernels  20.5 us (91%)
  local copies, waits for them, and re-layouts  1.23 us (5%)
  between operations  0.64 us (3%)
    pallas_call x1, Pallas kernels, on_device(): call(velocity, eddy_viscosity, cell_owner.reshape(16, LANES), cell_elemen...  20.5 us
    unnamed x1, local copies, waits for them, and re-layouts  0.62 us
    reshape x1, local copies, waits for them, and re-layouts, on_device(): moments = jnp.transpose(out[4:], (1, 0, 2)).reshape(1, 1, 4, 3, NODES)  0.61 us

profile of v3, /device:TPU:0, one launch (start us, length us, event | category | flops | bytes accessed | tf_op | source)
XLA Modules:
  0.0 22.3 jit_solution(9534997113434305080)
XLA Ops:
  0.6 20.5 %shard_map.86 = f32[7,4,512]{2,1,0:T(4,128)S(1)} custom-call(bf16[3,2,8,128]{3,2,1,0:T(8,128)(2,1)} %vel_hbm.1, f32[2,8,128]{2,1,0:T(8,128)} %visc_hbm.1, s32[16,128]{1,0:T(8,128)} %bitcast.13, s32[16,128]{1,0:T(8,128)} %bitcast.14, s32[16,128]{1,0:T(8,128)} %bitcast.15, f32[4,4,512]{2,1,0:T(4,128)} %bitcast.12, f32[168,256]{1,0:T(8,128)} %constant.2.clone.table_hbm), custom_call_target="tpu_custom_call" | custom-call | tf_op jit(solution)/shard_map/pallas_call | solution.py:473
  21.1 0.6 %slice_bitcast_fusion.1 = f32[1,1,4,3,512]{4,2,3,1,0:T(4,128)} fusion(f32[7,4,512]{2,1,0:T(4,128)S(1)} %shard_map.86), kind=kLoop, calls=%fused_computation.1 | loop fusion | bytes 49152 | tf_op jit(solution)/shard_map/reshape | solution.py:482
  21.7 0.6 %slice_bitcast_fusion = f32[4,1,1,4,512]{4,3,2,1,0:T(4,128)} fusion(f32[7,4,512]{2,1,0:T(4,128)S(1)} %shard_map.86), kind=kLoop, calls=%fused_computation | loop fusion | bytes 65536

commit v4 on v3

--- a/solution.py
+++ b/solution.py
@@ -118,8 +118,8 @@
             )
         )
     ]
-    for load in loads:
-        load.start()
+    for k in (1, 2, 3, 4, 5, 6, 0):
+        loads[k].start()
     pl.semaphore_wait(barrier, last + 2)
 
     def remote(src, dst, send_sem, recv_sem, device):
@@ -210,21 +210,15 @@
 
     basis = table_ref[160:168, :LANES]
 
-    def weights(step, carry):
-        for half in range(2):
-            row = 2 * step + half
-            position = jnp.broadcast_to(pos_ref[pl.ds(row, 1), :], (8, LANES))
-            along = [
-                jnp.take_along_axis(basis, index, axis=1, mode="promise_in_bounds")
-                for index in (position >> 8, (position >> 4) & 15, position & 15)
-            ]
-            pair = along[0][:, None, :] * along[1][None, :, :]
-            values = pair[:, :, None, :] * along[2][None, None, :, :]
-            columns = pl.ds(pl.multiple_of(row * LANES, LANES), LANES)
-            nodes[:, columns] = values.reshape(NODES, LANES).astype(jnp.bfloat16)
-        return carry
-
-    lax.fori_loop(0, 8, weights, 0)
+    for row in range(16):
+        position = jnp.broadcast_to(pos_ref[row:row + 1, :], (8, LANES))
+        along = [
+            jnp.take_along_axis(basis, index, axis=1, mode="promise_in_bounds")
+            for index in (position >> 8, (position >> 4) & 15, position & 15)
+        ]
+        pair = along[0][:, None, :] * along[1][None, :, :]
+        values = pair[:, :, None, :] * along[2][None, None, :, :]
+        nodes[:, LANES * row:LANES * (row + 1)] = values.reshape(NODES, LANES).astype(jnp.bfloat16)
 
     loads[3].wait()
     for c in range(4):

time: 22.5 us -> 22.5 us (level)
  no operation moved by 1% of the time
where the time goes in v4:
time: 22.5 us; the launch traced here: 22.3 us
  Pallas kernels  20.5 us (91%)
  local copies, waits for them, and re-layouts  1.23 us (5%)
  between operations  0.64 us (3%)
    pallas_call x1, Pallas kernels, on_device(): call(velocity, eddy_viscosity, cell_owner.reshape(16, LANES), cell_elemen...  20.5 us
    unnamed x1, local copies, waits for them, and re-layouts  0.62 us
    reshape x1, local copies, waits for them, and re-layouts, on_device(): moments = jnp.transpose(out[4:], (1, 0, 2)).reshape(1, 1, 4, 3, NODES)  0.61 us

profile of v4, /device:TPU:0, one launch (start us, length us, event | category | flops | bytes accessed | tf_op | source)
XLA Modules:
  0.0 22.3 jit_solution(12142236906995217855)
XLA Ops:
  0.6 20.5 %shard_map.86 = f32[7,4,512]{2,1,0:T(4,128)S(1)} custom-call(bf16[3,2,8,128]{3,2,1,0:T(8,128)(2,1)} %vel_hbm.1, f32[2,8,128]{2,1,0:T(8,128)} %visc_hbm.1, s32[16,128]{1,0:T(8,128)} %bitcast.13, s32[16,128]{1,0:T(8,128)} %bitcast.14, s32[16,128]{1,0:T(8,128)} %bitcast.15, f32[4,4,512]{2,1,0:T(4,128)} %bitcast.12, f32[168,256]{1,0:T(8,128)} %constant.2.clone.table_hbm), custom_call_target="tpu_custom_call" | custom-call | tf_op jit(solution)/shard_map/pallas_call | solution.py:467
  21.1 0.6 %slice_bitcast_fusion.1 = f32[1,1,4,3,512]{4,2,3,1,0:T(4,128)} fusion(f32[7,4,512]{2,1,0:T(4,128)S(1)} %shard_map.86), kind=kLoop, calls=%fused_computation.1 | loop fusion | bytes 49152 | tf_op jit(solution)/shard_map/reshape | solution.py:476
  21.7 0.6 %slice_bitcast_fusion = f32[4,1,1,4,512]{4,3,2,1,0:T(4,128)} fusion(f32[7,4,512]{2,1,0:T(4,128)S(1)} %shard_map.86), kind=kLoop, calls=%fused_computation | loop fusion | bytes 65536
